TPU v7x, 512 devices: a whole 4x4x16 slice. The times are simulated.
512 devices in a mesh: row: 32 (over z, x_lo), col: 16 (over y, x_hi, core).
Axes of the slice: x: 4 (x_hi: 2, x_lo: 2; x = x_hi * 2 + x_lo), y: 4, z: 16, core: 2. Of those that a mesh axis runs over, the one named last changes fastest.
Arguments:
- q_stream: bfloat16 [4096, 4096], P('col', 'row'), may hold values from -6 to 6
- k_stream: bfloat16 [4096, 4096], P('col', 'row'), may hold values from -6 to 6
- v_stream: bfloat16 [4096, 4096], P('col', 'row'), may hold values from -6 to 6
- long_filter: float32 [4096, 4096], P(('col', 'row')), may hold values from -1.3 to 1.3
- skip_gain: float32 [4096], P(('col', 'row')), may hold values from -4 to 4
- residual: bfloat16 [4096, 4096], P('col', 'row'), may hold values from -24 to 24
- norm_gain: float32 [4096], replicated, may hold values from 0.5 to 1.5
- w_out: bfloat16 [4096, 4096], P('row', 'col'), may hold values from -0.09375 to 0.09375
- w_gate: bfloat16 [4096, 8192], P('row', 'col'), may hold values from -0.09375 to 0.09375
- w_up: bfloat16 [4096, 8192], P('row', 'col'), may hold values from -0.09375 to 0.09375
- w_down: bfloat16 [8192, 4096], P('col'), may hold values from -0.09375 to 0.09375
Outputs:
- block_out: bfloat16 [4096, 4096], P('col', 'row')
All inputs are finite; a program needn't handle non-finite values.
Results may differ from a plain program's by a relative error of at most 0.015.
Values may be sent and summed in bfloat16 or wider, within the bound.
No kernel may reach another device: no remote copies, remote signals or barrier semaphores. Data moves between devices by JAX's collectives and lax.ppermute only.
A program may use at most 64 MiB of HBM per device.

v0:
```python
import math

import jax
import jax.numpy as jnp
from jax import lax
from jax.sharding import PartitionSpec as P

EPSILON = 1e-05
TWO_PI = 2.0 * math.pi


def contract(left_side, right_side):
    return lax.dot_general(
        left_side, right_side, (((0,), (0,)), ((), ())), preferred_element_type=jnp.float32
    )


def dft_tables(length):
    span = 2 * length
    tall = span // 128
    half_rows = length // 128
    k_first = jnp.arange(tall, dtype=jnp.int32)[:, None]
    n_first = jnp.arange(half_rows, dtype=jnp.int32)[None, :]
    angle_first = (k_first * n_first % tall).astype(jnp.float32) * (TWO_PI / tall)
    n_second = jnp.arange(128, dtype=jnp.int32)[None, :]
    angle_twist = (k_first * n_second % span).astype(jnp.float32) * (TWO_PI / span)
    k_second = jnp.arange(128, dtype=jnp.int32)
    angle_second = (k_second[:, None] * k_second[None, :] % 128).astype(jnp.float32) * (
        TWO_PI / 128
    )
    return (
        jnp.cos(angle_first),
        -jnp.sin(angle_first),
        jnp.cos(angle_twist),
        -jnp.sin(angle_twist),
        jnp.cos(angle_second),
        -jnp.sin(angle_second),
    )


def apply_first(matrix, blocks):
    return jnp.einsum("kn,cnm->ckm", matrix, blocks, precision=lax.Precision.HIGHEST)


def apply_last(blocks, matrix):
    return jnp.einsum("ckn,nm->ckm", blocks, matrix, precision=lax.Precision.HIGHEST)


def apply_back(matrix, blocks):
    return jnp.einsum("kn,ckm->cnm", matrix, blocks, precision=lax.Precision.HIGHEST)


def forward_dft(signal, tables):
    cos_first, sin_first, twist_re, twist_im, cos_second, sin_second = tables
    blocks = signal.reshape(signal.shape[0], signal.shape[1] // 128, 128)
    first_re = apply_first(cos_first, blocks)
    first_im = apply_first(sin_first, blocks)
    turned_re = first_re * twist_re - first_im * twist_im
    turned_im = first_re * twist_im + first_im * twist_re
    spec_re = apply_last(turned_re, cos_second) - apply_last(turned_im, sin_second)
    spec_im = apply_last(turned_re, sin_second) + apply_last(turned_im, cos_second)
    return (spec_re, spec_im)


def inverse_dft(spec_re, spec_im, tables, length):
    cos_first, sin_first, twist_re, twist_im, cos_second, sin_second = tables
    back_re = apply_last(spec_re, cos_second) + apply_last(spec_im, sin_second)
    back_im = apply_last(spec_im, cos_second) - apply_last(spec_re, sin_second)
    turned_re = back_re * twist_re + back_im * twist_im
    turned_im = back_im * twist_re - back_re * twist_im
    signal = (apply_back(cos_first, turned_re) + apply_back(sin_first, turned_im)) / (2.0 * length)
    return signal.reshape(signal.shape[0], length)


def on_device(
    q_stream,
    k_stream,
    v_stream,
    long_filter,
    skip_gain,
    residual,
    norm_gain,
    w_out,
    w_gate,
    w_up,
    w_down,
):
    rows_col = w_out.shape[1]
    query, keys_in, values_in = (
        lax.all_to_all(q_stream, "row", split_axis=0, concat_axis=1, tiled=True),
        lax.all_to_all(k_stream, "row", split_axis=0, concat_axis=1, tiled=True),
        lax.all_to_all(v_stream, "row", split_axis=0, concat_axis=1, tiled=True),
    )
    length = query.shape[1]
    tables = dft_tables(length)
    product = keys_in.astype(jnp.float32) * values_in.astype(jnp.float32)
    signal_re, signal_im = forward_dft(product, tables)
    filter_re, filter_im = forward_dft(long_filter, tables)
    joint_re = signal_re * filter_re - signal_im * filter_im
    joint_im = signal_re * filter_im + signal_im * filter_re
    convolved = inverse_dft(joint_re, joint_im, tables, length)
    gated = (query.astype(jnp.float32) * (convolved + skip_gain[:, None] * product)).astype(
        jnp.bfloat16
    )
    tile_cols = lax.all_to_all(gated, "row", split_axis=1, concat_axis=0, tiled=True)
    gated_full = lax.all_gather(tile_cols, "col", axis=0, tiled=True)
    part_rows = gated_full
    mixed_out = contract(lax.all_gather(w_out, "row", axis=0, tiled=True), part_rows)
    stream = (residual.astype(jnp.float32) + mixed_out).astype(jnp.bfloat16)
    width_all = norm_gain.shape[0]
    local_sum = jnp.sum(jnp.square(stream.astype(jnp.float32)), axis=0)
    power_sum = lax.psum(local_sum, "col")
    inverse_rms = lax.rsqrt(power_sum / width_all + EPSILON)
    gain_cols = lax.dynamic_slice_in_dim(norm_gain, lax.axis_index("col") * rows_col, rows_col, 0)
    normed = (stream.astype(jnp.float32) * inverse_rms[None, :] * gain_cols[:, None]).astype(
        jnp.bfloat16
    )
    normed_full = lax.all_gather(normed, "col", axis=0, tiled=True)
    part_rows = normed_full
    gate_proj = contract(lax.all_gather(w_gate, "row", axis=0, tiled=True), part_rows)
    up_proj = contract(lax.all_gather(w_up, "row", axis=0, tiled=True), part_rows)
    hidden = (jax.nn.silu(gate_proj) * up_proj).astype(jnp.bfloat16)
    down_out = lax.psum_scatter(
        contract(w_down, hidden).astype(jnp.bfloat16), "col", scatter_dimension=0, tiled=True
    ).astype(jnp.float32)
    return (stream.astype(jnp.float32) + down_out).astype(jnp.bfloat16)


def solution(mesh):
    placed = (
        P("col", "row"),
        P("col", "row"),
        P("col", "row"),
        P(("col", "row"), None),
        P(("col", "row")),
        P("col", "row"),
        P(),
        P("row", "col"),
        P("row", "col"),
        P("row", "col"),
        P("col", None),
    )
    return jax.shard_map(
        on_device, mesh=mesh, in_specs=placed, out_specs=P("col", "row"), check_vma=False
    )
```

profile of v0, /device:TPU:1, one launch (start us, length us, event | category | flops | bytes accessed | tf_op | source)
XLA Modules:
  0.0 748.7 jit_solution(10110213331254385598)
XLA Ops:
  6.5 0.0 copy-start
  6.5 17.1 %all-to-all-start.1 = ((bf16[32,8,128]{2,1,0:T(8,128)(2,1)}), bf16[32,8,128]{2,1,0:T(8,128)(2,1)S(1)}, u32[]{:S(2)}, u32[]{:S(2)}) async-start(bf16[32,8,128]{2,1,0:T(8,128)(2,1)} %bitcast.115), calls=%async_computation.1 | async-start | bytes 131072 | tf_op jit(solution)/shard_map/all_to_all | solution.py:91
  23.6 0.1 sine_negate_fusion.7
  23.8 0.0 copy-done
  23.8 0.5 fusion.36
  24.3 0.5 fusion.38
  24.8 0.6 fusion.15
  25.4 0.6 convolution_subtract_fusion.1
  26.1 10.2 %all-to-all-done.1 = bf16[32,8,128]{2,1,0:T(8,128)(2,1)S(1)} async-done(((bf16[32,8,128]{2,1,0:T(8,128)(2,1)}), bf16[32,8,128]{2,1,0:T(8,128)(2,1)S(1)}, u32[]{:S(2)}, u32[]{:S(2)}) %all-to-all-start.1) | async-done | bytes 65568 | tf_op jit(solution)/shard_map/all_to_all | solution.py:91
  36.3 3.9 all-to-all-start.2
  40.1 0.6 fusion.13
  40.8 0.6 convolution_add_fusion.1
  41.4 11.2 %all-to-all-done.2 = bf16[32,8,128]{2,1,0:T(8,128)(2,1)S(1)} async-done(((bf16[32,8,128]{2,1,0:T(8,128)(2,1)}), bf16[32,8,128]{2,1,0:T(8,128)(2,1)S(1)}, u32[]{:S(2)}, u32[]{:S(2)}) %all-to-all-start.2) | async-done | bytes 65568 | tf_op jit(solution)/shard_map/all_to_all | solution.py:92
  52.6 3.9 all-to-all-start
  56.5 0.0 all-gather.6.cloned.1.call-start
  56.5 0.5 convolution_bitcast_fusion.2
  57.1 0.5 convolution_bitcast_fusion.3
  57.5 0.0 copy-start.3
  57.6 0.6 fusion.57
  58.2 0.6 fusion.46
  58.8 0.0 copy-start.2
  58.8 0.6 convolution_subtract_fusion.2
  59.4 0.6 multiply_subtract_fusion
  60.1 0.6 fusion.52
  60.7 0.6 fusion.50
  61.3 0.6 convolution_add_fusion
  61.9 0.6 convolution_subtract_fusion
  62.6 0.4 fusion.25
  63.0 6.0 all-to-all-done
  69.0 0.0 copy-done.3
  69.0 0.4 fusion.8
  69.5 19.0 %all_to_all.55 = bf16[8,32,128]{2,0,1:T(8,128)(2,1)} all-to-all(bf16[8,32,128]{2,0,1:T(8,128)(2,1)S(1)} %copy.30), channel_id=1, replica_groups=mesh['row'=32,'col'=16] {'row'}, dimensions={1} | all-to-all | bytes 131072 | tf_op jit(solution)/shard_map/all_to_all | solution.py:105
  88.4 0.0 all-gather.6.cloned.1.call-update
  88.5 0.0 all-gather.8.cloned.1.call-start
  88.5 0.7 all-gather.8.cloned.1.call-update
  89.2 0.2 all-gather.10.cloned.1.call-start
  89.5 0.0 copy-done.2
  89.5 0.1 copy.24
  89.6 0.8 dynamic_slice.3
  90.3 54.8 %all-gather.6.cloned.1.call-done = bf16[4096,128]{1,0:T(8,128)(2,1)} async-done(((bf16[256,128]{1,0:T(8,128)(2,1)}), bf16[4096,128]{1,0:T(8,128)(2,1)}) %all-gather.6.cloned.1.call-update) | async-done | bytes 1048592 | tf_op jit(solution)/shard_map/all_gather | solution.py:106
  145.2 113.4 %all-gather.8.cloned.1.call-done = bf16[4096,256]{1,0:T(8,128)(2,1)} async-done(((bf16[128,256]{1,0:T(8,128)(2,1)}), bf16[4096,256]{1,0:T(8,128)(2,1)}) %all-gather.8.cloned.1.call-update) | async-done | bytes 2097168 | tf_op jit(solution)/shard_map/all_gather | solution.py:108
  258.6 2.5 multiply_reduce_fusion
  261.1 54.0 %psum.7 = f32[128]{0:T(128)S(1)} all-reduce(f32[128]{0:T(128)S(1)} %get-tuple-element.7), channel_id=1, replica_groups=mesh['row'=32,'col'=16] {'col'}, use_global_device_ids=true, to_apply=%region_1.2 | all-reduce | flops 128 | bytes 1024 | tf_op jit(solution)/shard_map/psum | solution.py:112
  315.1 0.7 multiply_convert_fusion
  315.9 0.0 all-gather.10.cloned.1.call-update
  315.9 0.0 all-gather.12.cloned.1.call-start
  315.9 0.5 all-gather.12.cloned.1.call-update
  316.5 0.0 all-gather.14.cloned.1.call-start
  316.5 0.5 all-gather.14.cloned.1.call-update
  317.0 0.0 reduce-scatter.2.cloned.1.call-start
  317.1 51.0 %all-gather.10.cloned.1.call-done = bf16[4096,128]{0,1:T(8,128)(2,1)} async-done(((bf16[256,128]{0,1:T(8,128)(2,1)}), bf16[4096,128]{0,1:T(8,128)(2,1)}) %all-gather.10.cloned.1.call-update) | async-done | bytes 1048592 | tf_op jit(solution)/shard_map/all_gather | solution.py:118
  368.1 0.0 copy-start.1
  368.1 123.7 %all-gather.12.cloned.1.call-done = bf16[4096,512]{1,0:T(8,128)(2,1)} async-done(((bf16[128,512]{1,0:T(8,128)(2,1)}), bf16[4096,512]{1,0:T(8,128)(2,1)}) %all-gather.12.cloned.1.call-update) | async-done | bytes 4194320 | tf_op jit(solution)/shard_map/all_gather | solution.py:120
  491.7 3.2 convolution_bitcast_fusion.1
  495.0 135.9 %all-gather.14.cloned.1.call-done = bf16[4096,512]{1,0:T(8,128)(2,1)} async-done(((bf16[128,512]{1,0:T(8,128)(2,1)}), bf16[4096,512]{1,0:T(8,128)(2,1)}) %all-gather.14.cloned.1.call-update) | async-done | bytes 4194320 | tf_op jit(solution)/shard_map/all_gather | solution.py:121
  630.9 0.0 copy-done.1
  630.9 5.8 fusion
  636.7 0.0 reduce-scatter.2.cloned.1.call-update
  636.8 103.5 %reduce-scatter.2.cloned.1.call-done = bf16[256,128]{0,1:T(8,128)(2,1)} async-done(((bf16[4096,128]{0,1:T(8,128)(2,1)}), bf16[256,128]{0,1:T(8,128)(2,1)}) %reduce-scatter.2.cloned.1.call-update) | async-done | bytes 65552 | tf_op jit(solution)/shard_map/reduce_scatter | solution.py:123
  740.2 0.9 add_convert_fusion
  741.1 0.7 copy.31
  (2 shorter events, 0.0 us)
Async XLA Ops:
  6.5 17.3 %copy-start = (f32[8,4096]{1,0:T(8,128)S(1)}, f32[8,4096]{1,0:T(8,128)}, u32[]{:S(2)}) copy-start(f32[8,4096]{1,0:T(8,128)} %param.14) | copy-start | bytes 393220
  6.5 29.7 %all-to-all-start.1 = ((bf16[32,8,128]{2,1,0:T(8,128)(2,1)}), bf16[32,8,128]{2,1,0:T(8,128)(2,1)S(1)}, u32[]{:S(2)}, u32[]{:S(2)}) async-start(bf16[32,8,128]{2,1,0:T(8,128)(2,1)} %bitcast.115), calls=%async_computation.1 | async-start | bytes 131072 | tf_op jit(solution)/shard_map/all_to_all | solution.py:91
  36.3 16.4 %all-to-all-start.2 = ((bf16[32,8,128]{2,1,0:T(8,128)(2,1)}), bf16[32,8,128]{2,1,0:T(8,128)(2,1)S(1)}, u32[]{:S(2)}, u32[]{:S(2)}) async-start(bf16[32,8,128]{2,1,0:T(8,128)(2,1)} %bitcast.116), calls=%async_computation.2 | async-start | bytes 131072 | tf_op jit(solution)/shard_map/all_to_all | solution.py:92
  52.6 16.4 %all-to-all-start = ((bf16[32,8,128]{2,1,0:T(8,128)(2,1)}), bf16[32,8,128]{2,1,0:T(8,128)(2,1)S(1)}, u32[]{:S(2)}, u32[]{:S(2)}) async-start(bf16[32,8,128]{2,1,0:T(8,128)(2,1)} %bitcast), calls=%async_computation | async-start | bytes 131072 | tf_op jit(solution)/shard_map/all_to_all | solution.py:90
  56.5 88.7 %all-gather.6.cloned.1.call-start = ((), (), s32[]{:S(2)}) async-start(), calls=%async_computation.5 | async-start | bytes 1114112 | tf_op jit(solution)/shard_map/all_gather | solution.py:106
  57.5 11.5 %copy-start.3 = (f32[8]{0:T(128)S(1)}, f32[8]{0:T(128)}, u32[]{:S(2)}) copy-start(f32[8]{0:T(128)} %param.15) | copy-start | bytes 100
  58.8 30.7 %copy-start.2 = (bf16[256,128]{1,0:T(8,128)(2,1)S(1)}, bf16[256,128]{1,0:T(8,128)(2,1)}, u32[]{:S(2)}) copy-start(bf16[256,128]{1,0:T(8,128)(2,1)} %param.16) | copy-start | bytes 196612
  88.5 170.1 %all-gather.8.cloned.1.call-start = ((), (), s32[]{:S(2)}) async-start(), calls=%async_computation.6 | async-start | bytes 2162688 | tf_op jit(solution)/shard_map/all_gather | solution.py:108
  89.2 278.8 %all-gather.10.cloned.1.call-start = ((), (), s32[]{:S(2)}) async-start(), calls=%async_computation.7 | async-start | bytes 1114112 | tf_op jit(solution)/shard_map/all_gather | solution.py:118
  315.9 175.8 %all-gather.12.cloned.1.call-start = ((), (), s32[]{:S(2)}) async-start(), calls=%async_computation.8 | async-start | bytes 4325376 | tf_op jit(solution)/shard_map/all_gather | solution.py:120
  316.5 314.4 %all-gather.14.cloned.1.call-start = ((), (), s32[]{:S(2)}) async-start(), calls=%async_computation.9 | async-start | bytes 4325376 | tf_op jit(solution)/shard_map/all_gather | solution.py:121
  317.0 423.2 %reduce-scatter.2.cloned.1.call-start = ((), (), s32[]{:S(2)}) async-start(), calls=%async_computation.10 | async-start | bytes 1114112 | tf_op jit(solution)/shard_map/reduce_scatter | solution.py:123
  368.1 262.8 %copy-start.1 = (bf16[4096,128]{0,1:T(8,128)(2,1)S(1)}, bf16[4096,128]{0,1:T(8,128)(2,1)}, u32[]{:S(2)}) copy-start(bf16[4096,128]{0,1:T(8,128)(2,1)} %all-gather.10.cloned.1.call-done) | copy-start | bytes 3145732
Sparse Core Ops, SparseCore 0:
  88.6 56.5 all-gather.5
  147.3 111.2 all-gather.7
  316.0 52.0 all-gather.9
  370.0 121.6 all-gather.11
  493.7 137.2 all-gather.13
  636.9 103.3 reduce-scatter.1
where the time goes:
time: 750 us; the launch traced here: 749 us
  waiting for transfers between devices  612 us (82%)
  blocking collectives  73 us (10%)
  starting transfers between devices  25.2 us (3%)
  matrix products  21.8 us (3%)
  between operations  13.7 us (2%)
    all_gather x1, waiting for transfers between devices, on_device(): lax.all_gather(w_up, 'row', axis=0, tiled=True)  136 us
    all_gather x1, waiting for transfers between devices, on_device(): lax.all_gather(w_gate, 'row', axis=0, tiled=True)  124 us
    all_gather x1, waiting for transfers between devices, on_device(): lax.all_gather(w_out, 'row', axis=0, tiled=True)  113 us
    reduce_scatter x1, waiting for transfers between devices, on_device(): lax.psum_scatter(contract(w_down, hidden).astype(jnp.bfloat16), 'col', sc...  103 us
    all_gather x1, waiting for transfers between devices, on_device(): gated_full = lax.all_gather(tile_cols, 'col', axis=0, tiled=True)  54.8 us
    psum x1, blocking collectives, on_device(): power_sum = lax.psum(local_sum, 'col')  54 us
    all_gather x1, waiting for transfers between devices, on_device(): normed_full = lax.all_gather(normed, 'col', axis=0, tiled=True)  51 us
    all_to_all x1, blocking collectives, on_device(): lax.all_to_all(gated, 'row', split_axis=1, concat_axis=0, tiled=True)  19 us
  transfers between devices with their start and end apart: 9, of which 9 were waited for; matrix products, arithmetic and copies ran while one was open for 2% of the time, Pallas kernels for 0%

commit v1 on v0

v1 whole, which is shorter than its diff:
```python
import math

import jax
import jax.numpy as jnp
from jax import lax
from jax.sharding import Mesh
from jax.sharding import PartitionSpec as P

EPSILON = 1e-05
TWO_PI = 2.0 * math.pi
ROW = ("z", "xl")
COL = ("y", "xh", "core")
PLANE = ("xl", "y", "xh", "core")


def contract(left_side, right_side):
    return lax.dot_general(
        left_side, right_side, (((0,), (0,)), ((), ())), preferred_element_type=jnp.float32
    )


def dft_tables(length):
    span = 2 * length
    tall = span // 128
    half_rows = length // 128
    k_first = jnp.arange(tall, dtype=jnp.int32)[:, None]
    n_first = jnp.arange(half_rows, dtype=jnp.int32)[None, :]
    angle_first = (k_first * n_first % tall).astype(jnp.float32) * (TWO_PI / tall)
    n_second = jnp.arange(128, dtype=jnp.int32)[None, :]
    angle_twist = (k_first * n_second % span).astype(jnp.float32) * (TWO_PI / span)
    k_second = jnp.arange(128, dtype=jnp.int32)
    angle_second = (k_second[:, None] * k_second[None, :] % 128).astype(jnp.float32) * (
        TWO_PI / 128
    )
    return (
        jnp.cos(angle_first),
        -jnp.sin(angle_first),
        jnp.cos(angle_twist),
        -jnp.sin(angle_twist),
        jnp.cos(angle_second),
        -jnp.sin(angle_second),
    )


def apply_first(matrix, blocks):
    return jnp.einsum("kn,cnm->ckm", matrix, blocks, precision=lax.Precision.HIGHEST)


def apply_last(blocks, matrix):
    return jnp.einsum("ckn,nm->ckm", blocks, matrix, precision=lax.Precision.HIGHEST)


def apply_back(matrix, blocks):
    return jnp.einsum("kn,ckm->cnm", matrix, blocks, precision=lax.Precision.HIGHEST)


def forward_dft(signal, tables):
    cos_first, sin_first, twist_re, twist_im, cos_second, sin_second = tables
    blocks = signal.reshape(signal.shape[0], signal.shape[1] // 128, 128)
    first_re = apply_first(cos_first, blocks)
    first_im = apply_first(sin_first, blocks)
    turned_re = first_re * twist_re - first_im * twist_im
    turned_im = first_re * twist_im + first_im * twist_re
    spec_re = apply_last(turned_re, cos_second) - apply_last(turned_im, sin_second)
    spec_im = apply_last(turned_re, sin_second) + apply_last(turned_im, cos_second)
    return (spec_re, spec_im)


def inverse_dft(spec_re, spec_im, tables, length):
    cos_first, sin_first, twist_re, twist_im, cos_second, sin_second = tables
    back_re = apply_last(spec_re, cos_second) + apply_last(spec_im, sin_second)
    back_im = apply_last(spec_im, cos_second) - apply_last(spec_re, sin_second)
    turned_re = back_re * twist_re + back_im * twist_im
    turned_im = back_im * twist_re - back_re * twist_im
    signal = (apply_back(cos_first, turned_re) + apply_back(sin_first, turned_im)) / (2.0 * length)
    return signal.reshape(signal.shape[0], length)


def to_plane(tile):
    halves = tile.reshape(2, 1, 128, 128)
    spread = jnp.broadcast_to(halves, (2, 16, 128, 128)).reshape(32, 128, 128)
    parts = lax.all_to_all(spread, PLANE, split_axis=0, concat_axis=0, tiled=True)
    return parts.reshape(2, 2048, 128)


def swap(array):
    return lax.ppermute(array, "xl", [(0, 1), (1, 0)])


def on_device(
    q_stream,
    k_stream,
    v_stream,
    long_filter,
    skip_gain,
    residual,
    norm_gain,
    w_out,
    w_gate,
    w_up,
    w_down,
):
    mine = lax.axis_index("xl")
    weights = lax.all_gather(
        jnp.concatenate([w_out, w_gate, w_up], axis=1), "z", axis=0, tiled=True
    )
    product = (k_stream.astype(jnp.float32) * v_stream.astype(jnp.float32)).astype(jnp.bfloat16)
    signal = lax.all_to_all(product, ROW, split_axis=0, concat_axis=1, tiled=True)
    length = signal.shape[1]
    tables = dft_tables(length)
    taps = jnp.concatenate([long_filter[:, :1] + skip_gain[:, None], long_filter[:, 1:]], axis=1)
    filter_re, filter_im = forward_dft(taps, tables)
    signal_re, signal_im = forward_dft(signal.astype(jnp.float32), tables)
    joint_re = signal_re * filter_re - signal_im * filter_im
    joint_im = signal_re * filter_im + signal_im * filter_re
    convolved = inverse_dft(joint_re, joint_im, tables, length).astype(jnp.bfloat16)
    convolved = lax.all_to_all(convolved, ROW, split_axis=1, concat_axis=0, tiled=True)
    gated = (q_stream.astype(jnp.float32) * convolved.astype(jnp.float32)).astype(jnp.bfloat16)
    gated_plane = to_plane(gated)
    weight_mix = weights[:, :256]
    far = contract(weight_mix, lax.dynamic_index_in_dim(gated_plane, 1 - mine, 0, keepdims=False))
    far = swap(far)
    near = contract(weight_mix, lax.dynamic_index_in_dim(gated_plane, mine, 0, keepdims=False))
    stream = (residual.astype(jnp.float32) + (near + far)).astype(jnp.bfloat16)
    stream_plane = to_plane(stream)
    wide = stream_plane.astype(jnp.float32)
    power = jnp.sum(jnp.square(wide), axis=1)
    gains = lax.dynamic_index_in_dim(norm_gain.reshape(16, 2, 128), mine, 1, keepdims=False)
    scaled = (wide * gains.reshape(1, 2048, 1)).astype(jnp.bfloat16)
    weight_ffw = weights[:, 256:]
    power_far = swap(lax.dynamic_index_in_dim(power, 1 - mine, 0, keepdims=False))
    far = contract(weight_ffw, lax.dynamic_index_in_dim(scaled, 1 - mine, 0, keepdims=False))
    far = swap(far.astype(jnp.bfloat16))
    near = contract(weight_ffw, lax.dynamic_index_in_dim(scaled, mine, 0, keepdims=False))
    power_sum = lax.dynamic_index_in_dim(power, mine, 0, keepdims=False) + power_far
    inverse_rms = lax.rsqrt(power_sum / norm_gain.shape[0] + EPSILON)
    both = (near + far.astype(jnp.float32)) * inverse_rms[None, :]
    hidden = (jax.nn.silu(both[:512]) * both[512:]).astype(jnp.bfloat16)
    down = contract(w_down, hidden).astype(jnp.bfloat16).reshape(16, 256, 128)
    parts = lax.all_to_all(down, COL, split_axis=0, concat_axis=0, tiled=True)
    down_out = jnp.sum(parts.astype(jnp.float32), axis=0)
    return (stream.astype(jnp.float32) + down_out).astype(jnp.bfloat16)


def solution(mesh):
    fine = Mesh(mesh.devices.reshape(16, 2, 4, 2, 2), ("z", "xl", "y", "xh", "core"))
    placed = (
        P(COL, ROW),
        P(COL, ROW),
        P(COL, ROW),
        P(COL + ROW, None),
        P(COL + ROW),
        P(COL, ROW),
        P(),
        P(ROW, COL),
        P(ROW, COL),
        P(ROW, COL),
        P(COL, None),
    )
    return jax.shard_map(
        on_device, mesh=fine, in_specs=placed, out_specs=P(COL, ROW), check_vma=False
    )
```

time: 750 us -> 180 us (0.24)
  waiting for transfers between devices: 612 us -> 47.8 us
  blocking collectives: 73 us -> 39.2 us
  starting transfers between devices: 25.2 us -> 49.7 us
    all_gather x5 -> x1, waiting for transfers between devices: 479 us -> 0.01 us  [on_device(): lax.all_gather(jnp.concatenate([w_out, w_gate, w_up], axis=1), 'z', axis=...]
    reduce_scatter x1 -> x0, waiting for transfers between devices: 103 us -> none  [on_device(): lax.psum_scatter(contract(w_down, hidden).astype(jnp.bfloat16), 'col', sc...]
    psum x1 -> x0, blocking collectives: 54 us -> none  [on_device(): power_sum = lax.psum(local_sum, 'col')]
    all_to_all x1 -> x2, blocking collectives: 19 us -> 39.2 us  [the longest x1 20.5 us: on_device(): parts = lax.all_to_all(down, COL, split_axis=0, concat_axis=0, tiled=True)]
    all_to_all x3, starting transfers between devices: 24.8 us -> 41.2 us  [the longest x2 24.3 us: to_plane(): lax.all_to_all(spread, PLANE, split_axis=0, concat_axis=0, tiled=True)]
    all_to_all x3, waiting for transfers between devices: 27.5 us -> 40.5 us  [the longest x2 34.1 us: to_plane(): lax.all_to_all(spread, PLANE, split_axis=0, concat_axis=0, tiled=True)]
    ppermute x0 -> x3, starting transfers between devices: none -> 8.47 us  [swap(): return lax.ppermute(array, 'xl', [(0, 1), (1, 0)])]
  transfers between devices with their start and end apart: 9 -> 7, of which waited for: 9 -> 5; matrix products, arithmetic and copies ran while one was open for 2% -> 9% of each run, Pallas kernels for 0% -> 0%
where the time goes in v1:
time: 180 us; the launch traced here: 179 us
  starting transfers between devices  49.7 us (28%)
  waiting for transfers between devices  47.8 us (27%)
  blocking collectives  39.2 us (22%)
  matrix products  16.8 us (9%)
  between operations  13.7 us (8%)
  local copies, waits for them, and re-layouts  6.24 us (3%)
  other arithmetic  5.79 us (3%)
    all_to_all x2, waiting for transfers between devices, to_plane(): lax.all_to_all(spread, PLANE, split_axis=0, concat_axis=0, tiled=True)  34.1 us
    all_to_all x2, starting transfers between devices, to_plane(): lax.all_to_all(spread, PLANE, split_axis=0, concat_axis=0, tiled=True)  24.3 us
    all_to_all x1, blocking collectives, on_device(): parts = lax.all_to_all(down, COL, split_axis=0, concat_axis=0, tiled=True)  20.5 us
    all_to_all x1, blocking collectives, on_device(): lax.all_to_all(convolved, ROW, split_axis=1, concat_axis=0, tiled=True)  18.7 us
    all_to_all x1, starting transfers between devices, on_device(): lax.all_to_all(product, ROW, split_axis=0, concat_axis=1, tiled=True)  17 us
    ppermute x3, starting transfers between devices, swap(): return lax.ppermute(array, 'xl', [(0, 1), (1, 0)])  8.47 us
    dot_general x12, matrix products, apply_last(): jnp.einsum('ckn,nm->ckm', blocks, matrix, precision=lax.Precision.HIGHEST)  7.42 us
    ppermute x3, waiting for transfers between devices, swap(): return lax.ppermute(array, 'xl', [(0, 1), (1, 0)])  7.3 us
  transfers between devices with their start and end apart: 7, of which 5 were waited for; matrix products, arithmetic and copies ran while one was open for 9% of the time, Pallas kernels for 0%

profile of v1, /device:TPU:1, one launch (start us, length us, event | category | flops | bytes accessed | tf_op | source)
XLA Modules:
  0.0 179.3 jit_solution(8968313881547712942)
XLA Ops:
  6.5 0.0 copy-start
  6.5 0.0 all-gather.2.cloned.1.call-start
  6.5 1.7 pad_maximum_fusion
  8.3 0.0 all-gather.2.cloned.1.call-update
  8.3 1.5 fusion.46
  9.8 17.0 %all-to-all-start = ((bf16[32,8,128]{2,1,0:T(8,128)(2,1)}), bf16[32,8,128]{2,1,0:T(8,128)(2,1)S(1)}, u32[]{:S(2)}, u32[]{:S(2)}) async-start(bf16[32,8,128]{2,1,0:T(8,128)(2,1)} %fusion.46), calls=%async_computation | async-start | bytes 131072 | tf_op jit(solution)/shard_map/all_to_all | solution.py:108
  26.8 0.7 slice.19
  27.5 1.0 slice.20
  28.5 0.1 copy.33
  28.6 0.7 bitcast_add_fusion
  29.2 0.1 copy.27
  29.3 0.1 sine_negate_fusion.7
  29.4 0.1 maximum_bitcast_fusion
  29.5 0.5 convolution_bitcast_fusion
  30.1 0.5 convolution_bitcast_fusion.1
  30.6 0.6 fusion.49
  31.2 0.6 convolution_add_fusion.1
  31.8 0.6 fusion.61
  32.4 0.6 convolution_subtract_fusion.1
  33.0 6.4 %all-to-all-done = bf16[32,8,128]{2,1,0:T(8,128)(2,1)S(1)} async-done(((bf16[32,8,128]{2,1,0:T(8,128)(2,1)}), bf16[32,8,128]{2,1,0:T(8,128)(2,1)S(1)}, u32[]{:S(2)}, u32[]{:S(2)}) %all-to-all-start) | async-done | bytes 65568 | tf_op jit(solution)/shard_map/all_to_all | solution.py:108
  39.4 0.4 convolution_bitcast_fusion.2
  39.8 0.4 convolution_bitcast_fusion.3
  40.2 0.6 fusion.51
  40.9 0.0 copy-start.2
  40.9 0.6 fusion.63
  41.5 0.6 convolution_subtract_fusion.2
  42.1 0.7 multiply_subtract_fusion
  42.8 0.6 fusion.57
  43.4 0.6 fusion.55
  44.0 0.0 copy-start.4
  44.0 0.6 convolution_add_fusion
  44.6 0.6 convolution_subtract_fusion
  45.3 0.4 fusion.28
  45.7 0.4 fusion.12
  46.1 18.7 %all_to_all.41 = bf16[8,32,128]{2,0,1:T(8,128)(2,1)S(1)} all-to-all(bf16[8,32,128]{2,0,1:T(8,128)(2,1)S(1)} %copy.28), channel_id=1, replica_groups=mesh['z'=16,'xl'=2,'y'=4,'xh'=2,'core'=2] {'z','xl'}, dimensions={1} | all-to-all | bytes 131072 | tf_op jit(solution)/shard_map/all_to_all | solution.py:117
  64.8 0.0 copy-done.2
  64.8 1.2 broadcast_in_dim.12
  66.1 9.9 %all-to-all-start.2 = ((bf16[32,128,128]{2,1,0:T(8,128)(2,1)}), bf16[32,128,128]{2,1,0:T(8,128)(2,1)S(1)}, u32[]{:S(2)}, u32[]{:S(2)}) async-start(bf16[32,128,128]{2,1,0:T(8,128)(2,1)} %bitcast.15), calls=%async_computation.2 | async-start | bytes 2097152 | tf_op jit(solution)/shard_map/all_to_all | solution.py:82
  75.9 17.1 %all-to-all-done.2 = bf16[32,128,128]{2,1,0:T(8,128)(2,1)S(1)} async-done(((bf16[32,128,128]{2,1,0:T(8,128)(2,1)}), bf16[32,128,128]{2,1,0:T(8,128)(2,1)S(1)}, u32[]{:S(2)}, u32[]{:S(2)}) %all-to-all-start.2) | async-done | bytes 1048608 | tf_op jit(solution)/shard_map/all_to_all | solution.py:82
  93.0 1.7 fusion.13
  94.7 2.9 %collective-permute-start = (f32[256,128]{1,0:T(8,128)S(1)}, f32[256,128]{1,0:T(8,128)S(1)}, u32[]{:S(2)}, u32[]{:S(2)}) collective-permute-start(f32[256,128]{1,0:T(8,128)S(1)} %fusion.13), channel_id=1, source_target_pairs={{0,16},{16,0},{1,17},{17,1},{2,18},{18,2},{3,19},{19,3},{4,20},{20... | collective-permute-start | bytes 393224 | tf_op jit(solution)/shard_map/ppermute | solution.py:87
  97.6 2.8 %collective-permute-done = f32[256,128]{1,0:T(8,128)S(1)} collective-permute-done((f32[256,128]{1,0:T(8,128)S(1)}, f32[256,128]{1,0:T(8,128)S(1)}, u32[]{:S(2)}, u32[]{:S(2)}) %collective-permute-start) | collective-permute-done | bytes 131104 | tf_op jit(solution)/shard_map/ppermute | solution.py:87
  100.4 0.0 copy-done.4
  100.4 1.7 fusion.11
  102.1 1.2 broadcast_in_dim.14
  103.4 14.4 %all-to-all-start.3 = ((bf16[32,128,128]{2,1,0:T(8,128)(2,1)}), bf16[32,128,128]{2,1,0:T(8,128)(2,1)S(1)}, u32[]{:S(2)}, u32[]{:S(2)}) async-start(bf16[32,128,128]{2,1,0:T(8,128)(2,1)} %bitcast.20), calls=%async_computation.3 | async-start | bytes 2097152 | tf_op jit(solution)/shard_map/all_to_all | solution.py:82
  117.8 17.0 %all-to-all-done.3 = bf16[32,128,128]{2,1,0:T(8,128)(2,1)S(1)} async-done(((bf16[32,128,128]{2,1,0:T(8,128)(2,1)}), bf16[32,128,128]{2,1,0:T(8,128)(2,1)S(1)}, u32[]{:S(2)}, u32[]{:S(2)}) %all-to-all-start.3) | async-done | bytes 1048608 | tf_op jit(solution)/shard_map/all_to_all | solution.py:82
  134.9 0.2 multiply_reduce_fusion
  135.1 0.2 convert_element_type.172
  135.4 0.3 fusion.4
  135.7 1.6 copy-done.3
  137.3 1.3 fusion.5
  138.7 0.0 copy-start.1
  138.7 2.2 %collective-permute-start.1 = (bf16[1024,128]{1,0:T(8,128)(2,1)S(1)}, bf16[1024,128]{1,0:T(8,128)(2,1)S(1)}, u32[]{:S(2)}, u32[]{:S(2)}) collective-permute-start(bf16[1024,128]{1,0:T(8,128)(2,1)S(1)} %fusion.5), channel_id=1, source_target_pairs={{0,16},{16,0},{1,17},{17,1},{2,18},{18,2},{3,19},{19,3},{4,20},{20... | collective-permute-start | bytes 786440 | tf_op jit(solution)/shard_map/ppermute | solution.py:87
  140.9 3.4 %collective-permute-start.2 = (f32[128]{0:T(128)S(1)}, f32[128]{0:T(128)S(1)}, u32[]{:S(2)}, u32[]{:S(2)}) collective-permute-start(f32[128]{0:T(128)S(1)} %fusion.134), channel_id=1, source_target_pairs={{0,16},{16,0},{1,17},{17,1},{2,18},{18,2},{3,19},{19,3},{4,20},{20... | collective-permute-start | bytes 1544 | tf_op jit(solution)/shard_map/ppermute | solution.py:87
  144.2 4.5 %collective-permute-done.2 = f32[128]{0:T(128)S(1)} collective-permute-done((f32[128]{0:T(128)S(1)}, f32[128]{0:T(128)S(1)}, u32[]{:S(2)}, u32[]{:S(2)}) %collective-permute-start.2) | collective-permute-done | bytes 544 | tf_op jit(solution)/shard_map/ppermute | solution.py:87
  148.8 0.0 collective-permute-done.1
  148.8 1.3 add_multiply_fusion
  150.1 0.8 convolution_convert_fusion
  150.9 0.1 copy.53
  151.0 20.5 %all_to_all.42 = bf16[16,256,128]{1,2,0:T(8,128)(2,1)S(1)} all-to-all(bf16[16,256,128]{1,2,0:T(8,128)(2,1)S(1)} %bitcast.124), channel_id=1, replica_groups=mesh['z'=16,'xl'=2,'y'=4,'xh'=2,'core'=2] {'y','xh','core'}, dimensions={0} | all-to-all | bytes 2097152 | tf_op jit(solution)/shard_map/all_to_all | solution.py:140
  171.5 0.1 convert_reduce_fusion
  171.7 0.1 copy.31
  171.8 0.7 add_convert_fusion
  (10 shorter events, 0.1 us)
Async XLA Ops:
  6.5 111.2 %copy-start = (f32[4096]{0:T(1024)S(1)}, f32[4096]{0:T(1024)}, u32[]{:S(2)}) copy-start(f32[4096]{0:T(1024)} %param.17) | copy-start | bytes 49156
  6.5 86.5 %all-gather.2.cloned.1.call-start = ((), (), s32[]{:S(2)}) async-start(), calls=%async_computation.5 | async-start | bytes 5570560 | tf_op jit(solution)/shard_map/all_gather | solution.py:104
  9.8 29.6 %all-to-all-start = ((bf16[32,8,128]{2,1,0:T(8,128)(2,1)}), bf16[32,8,128]{2,1,0:T(8,128)(2,1)S(1)}, u32[]{:S(2)}, u32[]{:S(2)}) async-start(bf16[32,8,128]{2,1,0:T(8,128)(2,1)} %fusion.46), calls=%async_computation | async-start | bytes 131072 | tf_op jit(solution)/shard_map/all_to_all | solution.py:108
  40.9 23.9 %copy-start.2 = (bf16[256,128]{1,0:T(8,128)(2,1)S(1)}, bf16[256,128]{1,0:T(8,128)(2,1)}, u32[]{:S(2)}) copy-start(bf16[256,128]{1,0:T(8,128)(2,1)} %param.11) | copy-start | bytes 196612
  44.0 56.4 %copy-start.4 = (bf16[256,128]{1,0:T(8,128)(2,1)S(1)}, bf16[256,128]{1,0:T(8,128)(2,1)}, u32[]{:S(2)}) copy-start(bf16[256,128]{1,0:T(8,128)(2,1)} %param.16) | copy-start | bytes 196612
  66.1 26.9 %all-to-all-start.2 = ((bf16[32,128,128]{2,1,0:T(8,128)(2,1)}), bf16[32,128,128]{2,1,0:T(8,128)(2,1)S(1)}, u32[]{:S(2)}, u32[]{:S(2)}) async-start(bf16[32,128,128]{2,1,0:T(8,128)(2,1)} %bitcast.15), calls=%async_computation.2 | async-start | bytes 2097152 | tf_op jit(solution)/shard_map/all_to_all | solution.py:82
  94.7 5.7 %collective-permute-start = (f32[256,128]{1,0:T(8,128)S(1)}, f32[256,128]{1,0:T(8,128)S(1)}, u32[]{:S(2)}, u32[]{:S(2)}) collective-permute-start(f32[256,128]{1,0:T(8,128)S(1)} %fusion.13), channel_id=1, source_target_pairs={{0,16},{16,0},{1,17},{17,1},{2,18},{18,2},{3,19},{19,3},{4,20},{20... | collective-permute-start | bytes 393224 | tf_op jit(solution)/shard_map/ppermute | solution.py:87
  103.4 31.5 %all-to-all-start.3 = ((bf16[32,128,128]{2,1,0:T(8,128)(2,1)}), bf16[32,128,128]{2,1,0:T(8,128)(2,1)S(1)}, u32[]{:S(2)}, u32[]{:S(2)}) async-start(bf16[32,128,128]{2,1,0:T(8,128)(2,1)} %bitcast.20), calls=%async_computation.3 | async-start | bytes 2097152 | tf_op jit(solution)/shard_map/all_to_all | solution.py:82
  134.9 2.5 %copy-start.3 = (bf16[2048,1280]{1,0:T(8,128)(2,1)S(1)}, bf16[2048,1280]{1,0:T(8,128)(2,1)}, u32[]{:S(2)}) copy-start(bf16[2048,1280]{1,0:T(8,128)(2,1)} %all-gather.2.cloned.1.call-done) | copy-start | bytes 15728644
  138.7 11.4 %copy-start.1 = (bf16[512,4096]{1,0:T(8,128)(2,1)S(1)}, bf16[512,4096]{1,0:T(8,128)(2,1)}, u32[]{:S(2)}) copy-start(bf16[512,4096]{1,0:T(8,128)(2,1)} %param.21) | copy-start | bytes 12582916
  138.7 10.1 %collective-permute-start.1 = (bf16[1024,128]{1,0:T(8,128)(2,1)S(1)}, bf16[1024,128]{1,0:T(8,128)(2,1)S(1)}, u32[]{:S(2)}, u32[]{:S(2)}) collective-permute-start(bf16[1024,128]{1,0:T(8,128)(2,1)S(1)} %fusion.5), channel_id=1, source_target_pairs={{0,16},{16,0},{1,17},{17,1},{2,18},{18,2},{3,19},{19,3},{4,20},{20... | collective-permute-start | bytes 786440 | tf_op jit(solution)/shard_map/ppermute | solution.py:87
  140.9 7.9 %collective-permute-start.2 = (f32[128]{0:T(128)S(1)}, f32[128]{0:T(128)S(1)}, u32[]{:S(2)}, u32[]{:S(2)}) collective-permute-start(f32[128]{0:T(128)S(1)} %fusion.134), channel_id=1, source_target_pairs={{0,16},{16,0},{1,17},{17,1},{2,18},{18,2},{3,19},{19,3},{4,20},{20... | collective-permute-start | bytes 1544 | tf_op jit(solution)/shard_map/ppermute | solution.py:87
Sparse Core Ops, SparseCore 0:
  9.4 83.0 all-gather.1

commit v2 on v1

--- a/solution.py
+++ b/solution.py
@@ -3,6 +3,8 @@
 import jax
 import jax.numpy as jnp
 from jax import lax
+from jax.experimental import pallas as pl
+from jax.experimental.pallas import tpu as pltpu
 from jax.sharding import Mesh
 from jax.sharding import PartitionSpec as P
 
@@ -10,13 +12,6 @@
 TWO_PI = 2.0 * math.pi
 ROW = ("z", "xl")
 COL = ("y", "xh", "core")
-PLANE = ("xl", "y", "xh", "core")
-
-
-def contract(left_side, right_side):
-    return lax.dot_general(
-        left_side, right_side, (((0,), (0,)), ((), ())), preferred_element_type=jnp.float32
-    )
 
 
 def dft_tables(length):
@@ -76,15 +71,117 @@
     return signal.reshape(signal.shape[0], length)
 
 
+def swap(array, axis):
+    return lax.ppermute(array, axis, [(0, 1), (1, 0)])
+
+
+def after(array, *others):
+    return lax.optimization_barrier((array,) + others)[0]
+
+
 def to_plane(tile):
-    halves = tile.reshape(2, 1, 128, 128)
-    spread = jnp.broadcast_to(halves, (2, 16, 128, 128)).reshape(32, 128, 128)
-    parts = lax.all_to_all(spread, PLANE, split_axis=0, concat_axis=0, tiled=True)
-    return parts.reshape(2, 2048, 128)
-
-
-def swap(array):
-    return lax.ppermute(array, "xl", [(0, 1), (1, 0)])
+    halves = tile.reshape(128, 2, 128).transpose(1, 0, 2)[:, None]
+    spread = jnp.broadcast_to(halves, (2, 8, 128, 128)).reshape(16, 128, 128)
+    return lax.all_to_all(spread, ("xl", "y", "xh"), split_axis=0, concat_axis=0, tiled=True)
+
+
+def both_tiles(parts_ref, side, index):
+    far, near = (1 - side) * 8, side * 8
+    return jnp.concatenate(
+        [
+            jnp.concatenate([parts_ref[far + index + i], parts_ref[near + index + i]], axis=0)
+            for i in range(2)
+        ],
+        axis=1,
+    )
+
+
+def mix_kernel(where_ref, own_ref, other_ref, w_own_ref, w_other_ref, far_ref, near_ref):
+    side = where_ref[1]
+    total = jnp.zeros((256, 256), jnp.float32)
+    for parts_ref, w_ref in ((own_ref, w_own_ref), (other_ref, w_other_ref)):
+        for i in range(4):
+            total += jnp.dot(
+                both_tiles(parts_ref, side, 2 * i),
+                w_ref[2 * i : 2 * i + 2].reshape(256, 256),
+                preferred_element_type=jnp.float32,
+            )
+    far_ref[...] = total[:128]
+    near_ref[...] = total[128:]
+
+
+def half_ffw(side, parts_ref, gain_ref, w_ref):
+    total = jnp.zeros((256, 1024), jnp.float32)
+    power = jnp.zeros((256, 1), jnp.float32)
+    for i in range(4):
+        wide = both_tiles(parts_ref, side, 2 * i).astype(jnp.float32)
+        power += jnp.sum(wide * wide, axis=1, keepdims=True)
+        scaled = wide * gain_ref[:, i * 256 : i * 256 + 256]
+        total += jnp.dot(
+            scaled.astype(jnp.bfloat16),
+            w_ref[2 * i : 2 * i + 2].reshape(256, 1024),
+            preferred_element_type=jnp.float32,
+        )
+    return total, jnp.broadcast_to(power, (256, 128))
+
+
+def first_kernel(where_ref, parts_ref, gain_ref, w_ref, total_ref, power_ref):
+    total, power = half_ffw(where_ref[1], parts_ref, gain_ref, w_ref)
+    total_ref[...] = total
+    power_ref[...] = power
+
+
+def second_kernel(
+    where_ref, parts_ref, gain_ref, begun_ref, power_ref, w_ref, far_ref, near_ref, own_power_ref
+):
+    total, power = half_ffw(where_ref[1], parts_ref, gain_ref, w_ref)
+    total += begun_ref[...]
+    power += power_ref[...]
+    far_ref[:128] = total[:128].astype(jnp.bfloat16)
+    row = power[:128].T[:16]
+    high = row.astype(jnp.bfloat16)
+    low = (row - high.astype(jnp.float32)).astype(jnp.bfloat16)
+    pair = jnp.concatenate([high, low], axis=1)
+    far_ref[128:] = jnp.concatenate([pair, pair, pair, pair], axis=1)
+    near_ref[...] = total[128:]
+    own_power_ref[...] = power[128:]
+
+
+def columns_of(w_ref, index, core):
+    return w_ref[:, pl.ds(pl.multiple_of((2 * index + core) * 256, 256), 256)]
+
+
+def down_far_kernel(where_ref, near_ref, far_ref, power_ref, w_ref, out_ref, hidden_ref):
+    sums = far_ref[128:].astype(jnp.float32)
+    sums = jnp.broadcast_to(sums[:1, :128] + sums[:1, 128:256], (128, 128)).T
+    inverse_rms = lax.rsqrt((power_ref[:, :1] + sums[:, :1]) / 4096 + EPSILON)
+    both = (near_ref[...] + far_ref[:128].astype(jnp.float32)) * inverse_rms
+    hidden = (jax.nn.silu(both[:, :512]) * both[:, 512:]).astype(jnp.bfloat16)
+    hidden_ref[...] = hidden
+    for i in range(8):
+        out_ref[i] = jnp.dot(
+            hidden, columns_of(w_ref, i, 1 - where_ref[0]), preferred_element_type=jnp.float32
+        ).astype(jnp.bfloat16)
+
+
+def down_near_kernel(where_ref, hidden_ref, w_ref, out_ref):
+    for i in range(8):
+        out_ref[i] = jnp.dot(
+            hidden_ref[...], columns_of(w_ref, i, where_ref[0]), preferred_element_type=jnp.float32
+        )
+
+
+def local_call(kernel, where, operands, outs, flops):
+    outs = [jax.ShapeDtypeStruct(shape, dtype) for shape, dtype in outs]
+    return pl.pallas_call(
+        kernel,
+        in_specs=[pl.BlockSpec(memory_space=pltpu.SMEM)]
+        + [pl.BlockSpec(memory_space=pltpu.VMEM)] * len(operands),
+        out_specs=[pl.BlockSpec(memory_space=pltpu.VMEM)] * len(outs),
+        out_shape=outs,
+        compiler_params=pltpu.CompilerParams(vmem_limit_bytes=16 * 1024 * 1024),
+        cost_estimate=pl.CostEstimate(flops=flops, bytes_accessed=2**21, transcendentals=0),
+    )(where, *operands)
 
 
 def on_device(
@@ -100,10 +197,17 @@
     w_up,
     w_down,
 ):
-    mine = lax.axis_index("xl")
+    side = lax.axis_index("xl")
+    core = lax.axis_index("core")
+    where = jnp.stack([core, side]).astype(jnp.int32)
     weights = lax.all_gather(
-        jnp.concatenate([w_out, w_gate, w_up], axis=1), "z", axis=0, tiled=True
-    )
+        jnp.concatenate([w_gate, w_up, w_out], axis=1), "z", axis=0, tiled=True
+    ).reshape(8, 2, 128, 1280)
+
+    def rows_of(gathered, owner, start, width):
+        part = lax.dynamic_slice(gathered, (0, owner, 0, start), (8, 1, 128, width))
+        return part.reshape(8, 128, width)
+
     product = (k_stream.astype(jnp.float32) * v_stream.astype(jnp.float32)).astype(jnp.bfloat16)
     signal = lax.all_to_all(product, ROW, split_axis=0, concat_axis=1, tiled=True)
     length = signal.shape[1]
@@ -116,30 +220,67 @@
     convolved = inverse_dft(joint_re, joint_im, tables, length).astype(jnp.bfloat16)
     convolved = lax.all_to_all(convolved, ROW, split_axis=1, concat_axis=0, tiled=True)
     gated = (q_stream.astype(jnp.float32) * convolved.astype(jnp.float32)).astype(jnp.bfloat16)
-    gated_plane = to_plane(gated)
-    weight_mix = weights[:, :256]
-    far = contract(weight_mix, lax.dynamic_index_in_dim(gated_plane, 1 - mine, 0, keepdims=False))
-    far = swap(far)
-    near = contract(weight_mix, lax.dynamic_index_in_dim(gated_plane, mine, 0, keepdims=False))
-    stream = (residual.astype(jnp.float32) + (near + far)).astype(jnp.bfloat16)
-    stream_plane = to_plane(stream)
-    wide = stream_plane.astype(jnp.float32)
-    power = jnp.sum(jnp.square(wide), axis=1)
-    gains = lax.dynamic_index_in_dim(norm_gain.reshape(16, 2, 128), mine, 1, keepdims=False)
-    scaled = (wide * gains.reshape(1, 2048, 1)).astype(jnp.bfloat16)
-    weight_ffw = weights[:, 256:]
-    power_far = swap(lax.dynamic_index_in_dim(power, 1 - mine, 0, keepdims=False))
-    far = contract(weight_ffw, lax.dynamic_index_in_dim(scaled, 1 - mine, 0, keepdims=False))
-    far = swap(far.astype(jnp.bfloat16))
-    near = contract(weight_ffw, lax.dynamic_index_in_dim(scaled, mine, 0, keepdims=False))
-    power_sum = lax.dynamic_index_in_dim(power, mine, 0, keepdims=False) + power_far
-    inverse_rms = lax.rsqrt(power_sum / norm_gain.shape[0] + EPSILON)
-    both = (near + far.astype(jnp.float32)) * inverse_rms[None, :]
-    hidden = (jax.nn.silu(both[:512]) * both[512:]).astype(jnp.bfloat16)
-    down = contract(w_down, hidden).astype(jnp.bfloat16).reshape(16, 256, 128)
-    parts = lax.all_to_all(down, COL, split_axis=0, concat_axis=0, tiled=True)
+    own = to_plane(gated.T)
+    other = swap(own, "core")
+    far, near = local_call(
+        mix_kernel,
+        where,
+        (own, other, rows_of(weights, core, 1024, 256), rows_of(weights, 1 - core, 1024, 256)),
+        [((128, 256), jnp.float32)] * 2,
+        2 * 256 * 256 * 2048,
+    )
+    weights = after(weights, near)
+    w_own, w_other = rows_of(weights, core, 0, 1024), rows_of(weights, 1 - core, 0, 1024)
+    far = swap(far, "xl")
+    far = after(far, w_own, w_other)
+    stream = (residual.T.astype(jnp.float32) + (near + far)).astype(jnp.bfloat16)
+    own = to_plane(stream)
+    other = swap(own, "core")
+    gains = lax.dynamic_index_in_dim(norm_gain.reshape(8, 2, 2, 128), side, 2, keepdims=False)
+    gain_own = lax.dynamic_index_in_dim(gains, core, 1, keepdims=False).reshape(1, 1024)
+    gain_other = lax.dynamic_index_in_dim(gains, 1 - core, 1, keepdims=False).reshape(1, 1024)
+    begun, power = local_call(
+        first_kernel,
+        where,
+        (own, gain_own, w_own),
+        [((256, 1024), jnp.float32), ((256, 128), jnp.float32)],
+        2 * 256 * 1024 * 1024,
+    )
+    other = after(other, begun)
+    far, near, power = local_call(
+        second_kernel,
+        where,
+        (other, gain_other, begun, power, w_other),
+        [((144, 1024), jnp.bfloat16), ((128, 1024), jnp.float32), ((128, 128), jnp.float32)],
+        2 * 256 * 1024 * 1024,
+    )
+    far = swap(far, "xl")
+    far, hidden = local_call(
+        down_far_kernel,
+        where,
+        (near, far, power, w_down),
+        [((8, 128, 256), jnp.bfloat16), ((128, 512), jnp.bfloat16)],
+        2 * 128 * 512 * 2048,
+    )
+    far = swap(far, "core")
+    (near,) = local_call(
+        down_near_kernel,
+        where,
+        (hidden, w_down),
+        [((8, 128, 256), jnp.float32)],
+        2 * 128 * 512 * 2048,
+    )
+    far = after(far, near)
+    down = (near + far.astype(jnp.float32)).astype(jnp.bfloat16)
+    parts = lax.all_to_all(
+        down,
+        ("y", "xh"),
+        split_axis=0,
+        concat_axis=0,
+        tiled=True,
+    )
     down_out = jnp.sum(parts.astype(jnp.float32), axis=0)
-    return (stream.astype(jnp.float32) + down_out).astype(jnp.bfloat16)
+    return (stream.astype(jnp.float32) + down_out).astype(jnp.bfloat16).T
 
 
 def solution(mesh):

time: 180 us -> 170 us (0.944)
  waiting for transfers between devices: 47.8 us -> 21.2 us
  blocking collectives: 39.2 us -> 62.3 us
  starting transfers between devices: 49.7 us -> 41.5 us
  matrix products: 16.8 us -> 10 us
  Pallas kernels: 0 us -> 5.66 us
  local copies, waits for them, and re-layouts: 6.24 us -> 10.3 us
    all_to_all x2 -> x0, waiting for transfers between devices: 34.1 us -> none  [to_plane(): lax.all_to_all(spread, PLANE, split_axis=0, concat_axis=0, tiled=True)]
    all_to_all x2 -> x0, starting transfers between devices: 24.3 us -> none  [to_plane(): lax.all_to_all(spread, PLANE, split_axis=0, concat_axis=0, tiled=True)]
    all_to_all x1 -> x3, blocking collectives: 20.5 us -> 43.1 us  [the longest x2 29.5 us: to_plane(): lax.all_to_all(spread, ('xl', 'y', 'xh'), split_axis=0, concat_axis=0, ti...]
    ppermute x3 -> x5, starting transfers between devices: 8.47 us -> 24.5 us  [swap(): return lax.ppermute(array, axis, [(0, 1), (1, 0)])]
    dot_general x5 -> x0, matrix products: 6.8 us -> none  [contract(): lax.dot_general(left_side, right_side, (((0,), (0,)), ((), ())), preferre...]
    all_gather x1, waiting for transfers between devices: 0.01 us -> 6.04 us  [on_device(): lax.all_gather(jnp.concatenate([w_gate, w_up, w_out], axis=1), 'z', axis=...]
    pallas_call x0 -> x5, Pallas kernels: none -> 5.66 us  [local_call(): pl.pallas_call(kernel, in_specs=[pl.BlockSpec(memory_space=pltpu.SMEM)] +...]
    reshape x1 -> x4, local copies, waits for them, and re-layouts: 0.1 us -> 5.45 us  [the longest x2 5.41 us: rows_of(): return part.reshape(8, 128, width)]
  transfers between devices with their start and end apart: 7 -> 7, of which waited for: 5 -> 4; matrix products, arithmetic and copies ran while one was open for 9% -> 12% of each run, Pallas kernels for 0% -> 1%
where the time goes in v2:
time: 170 us; the launch traced here: 169 us
  blocking collectives  62.3 us (37%)
  starting transfers between devices  41.5 us (24%)
  waiting for transfers between devices  21.2 us (12%)
  between operations  13.8 us (8%)
  local copies, waits for them, and re-layouts  10.3 us (6%)
  matrix products  10 us (6%)
  Pallas kernels  5.66 us (3%)
  other arithmetic  4.54 us (3%)
    all_to_all x2, blocking collectives, to_plane(): lax.all_to_all(spread, ('xl', 'y', 'xh'), split_axis=0, concat_axis=0, ti...  29.5 us
    ppermute x5, starting transfers between devices, swap(): return lax.ppermute(array, axis, [(0, 1), (1, 0)])  24.5 us
    all_to_all x1, blocking collectives, on_device(): lax.all_to_all(convolved, ROW, split_axis=1, concat_axis=0, tiled=True)  19.2 us
    all_to_all x1, starting transfers between devices, on_device(): lax.all_to_all(product, ROW, split_axis=0, concat_axis=1, tiled=True)  17 us
    all_to_all x1, blocking collectives, on_device(): lax.all_to_all(down, ('y', 'xh'), split_axis=0, concat_axis=0, tiled=True)  13.5 us
    ppermute x5, waiting for transfers between devices, swap(): return lax.ppermute(array, axis, [(0, 1), (1, 0)])  8.83 us
    dot_general x12, matrix products, apply_last(): jnp.einsum('ckn,nm->ckm', blocks, matrix, precision=lax.Precision.HIGHEST)  7.43 us
    all_to_all x1, waiting for transfers between devices, on_device(): lax.all_to_all(product, ROW, split_axis=0, concat_axis=1, tiled=True)  6.34 us
  transfers between devices with their start and end apart: 7, of which 4 were waited for; matrix products, arithmetic and copies ran while one was open for 12% of the time, Pallas kernels for 1%

profile of v2, /device:TPU:1, one launch (start us, length us, event | category | flops | bytes accessed | tf_op | source)
XLA Modules:
  0.0 169.3 jit_solution(9530295123472546061)
XLA Ops:
  6.5 1.8 %pad_maximum_fusion = bf16[128,1280]{1,0:T(8,128)(2,1)} fusion(bf16[128,256]{1,0:T(8,128)(2,1)} %param.18, bf16[128,512]{1,0:T(8,128)(2,1)} %param.20, bf16[128,512]{1,0:T(8,128)(2,1)} %param.19), kind=kLoop, calls=%fused_computation.20 | loop fusion | flops 983040 | bytes 655360 | tf_op jit(solution)/shard_map/concatenate | solution.py:204
  8.3 0.0 all-gather.2.cloned.1.call-update
  8.3 1.5 fusion.23
  9.8 17.0 %all-to-all-start = ((bf16[32,8,128]{2,1,0:T(8,128)(2,1)}), bf16[32,8,128]{2,1,0:T(8,128)(2,1)S(1)}, u32[]{:S(2)}, u32[]{:S(2)}) async-start(bf16[32,8,128]{2,1,0:T(8,128)(2,1)} %fusion.23), calls=%async_computation | async-start | bytes 131072 | tf_op jit(solution)/shard_map/all_to_all | solution.py:212
  26.8 1.0 slice.7
  27.8 0.7 slice.6
  28.5 0.1 copy.46
  28.6 0.7 bitcast_add_fusion.1
  29.2 0.1 copy.37
  29.3 0.1 sine_negate_fusion.7
  29.5 0.1 maximum_bitcast_fusion
  29.6 0.5 convolution_bitcast_fusion
  30.1 0.5 convolution_bitcast_fusion.1
  30.6 0.6 fusion.39
  31.2 0.6 convolution_subtract_fusion.1
  31.8 0.6 fusion.27
  32.5 0.6 convolution_add_fusion.1
  33.1 0.0 copy-start.2
  33.1 6.3 %all-to-all-done = bf16[32,8,128]{2,1,0:T(8,128)(2,1)S(1)} async-done(((bf16[32,8,128]{2,1,0:T(8,128)(2,1)}), bf16[32,8,128]{2,1,0:T(8,128)(2,1)S(1)}, u32[]{:S(2)}, u32[]{:S(2)}) %all-to-all-start) | async-done | bytes 65568 | tf_op jit(solution)/shard_map/all_to_all | solution.py:212
  39.4 0.4 convolution_bitcast_fusion.2
  39.8 0.4 convolution_bitcast_fusion.3
  40.2 0.6 fusion.41
  40.9 0.0 copy-start.3
  40.9 0.6 fusion.29
  41.5 0.6 convolution_subtract_fusion.2
  42.1 0.7 multiply_subtract_fusion
  42.8 0.6 fusion.35
  43.4 0.6 fusion.33
  44.0 0.6 convolution_add_fusion
  44.6 0.6 convolution_subtract_fusion
  45.3 0.4 fusion.6
  45.7 0.4 fusion.2
  46.1 19.2 %all_to_all.41 = bf16[8,32,128]{2,0,1:T(8,128)(2,1)S(1)} all-to-all(bf16[8,32,128]{2,0,1:T(8,128)(2,1)S(1)} %copy.38), channel_id=1, replica_groups=mesh['z'=16,'xl'=2,'y'=4,'xh'=2,'core'=2] {'z','xl'}, dimensions={1} | all-to-all | bytes 131072 | tf_op jit(solution)/shard_map/all_to_all | solution.py:221
  65.4 0.1 copy.39
  65.5 0.1 broadcast_in_dim.7
  65.6 15.4 %all_to_all.42.own_ref = bf16[16,128,128]{2,1,0:T(8,128)(2,1)S(1)} all-to-all(bf16[16,128,128]{2,1,0:T(8,128)(2,1)S(1)} %bitcast.114), channel_id=1, replica_groups=mesh['z'=16,'xl'=2,'y'=4,'xh'=2,'core'=2] {'xl','y','xh'}, dimensions={0} | all-to-all | bytes 1048576 | tf_op jit(solution)/shard_map/all_to_all | solution.py:85
  81.0 5.3 %collective-permute-start = (bf16[16,128,128]{2,1,0:T(8,128)(2,1)S(1)}, bf16[16,128,128]{2,1,0:T(8,128)(2,1)S(1)}, u32[]{:S(2)}, u32[]{:S(2)}) collective-permute-start(bf16[16,128,128]{2,1,0:T(8,128)(2,1)S(1)} %all_to_all.42.own_ref), channel_id=1, source_target_pairs={{0,1},{1,0},{2,3},{3,2},{4,5},{5,4},{6,7},{7,6},{8,9},{9,8},{10,11... | collective-permute-start | bytes 1572872 | tf_op jit(solution)/shard_map/ppermute | solution.py:75
  86.3 0.1 copy.34
  86.5 0.1 pad_add_fusion.where_ref
  86.5 6.0 %all-gather.2.cloned.1.call-done = bf16[2048,1280]{1,0:T(8,128)(2,1)} async-done(((bf16[128,1280]{1,0:T(8,128)(2,1)}), bf16[2048,1280]{1,0:T(8,128)(2,1)}) %all-gather.2.cloned.1.call-update) | async-done | bytes 5242896 | tf_op jit(solution)/shard_map/all_gather | solution.py:203
  92.6 1.3 dynamic-slice_bitcast_fusion.2
  93.9 0.0 collective-permute-done.other_ref
  93.9 1.0 shard_map.109
  94.9 0.0 copy-start.4
  94.9 3.3 %collective-permute-start.1 = (f32[128,256]{1,0:T(8,128)S(1)}, f32[128,256]{1,0:T(8,128)S(1)}, u32[]{:S(2)}, u32[]{:S(2)}) collective-permute-start(f32[128,256]{1,0:T(8,128)S(1)} %get-tuple-element.19), channel_id=1, source_target_pairs={{0,16},{16,0},{1,17},{17,1},{2,18},{18,2},{3,19},{19,3},{4,20},{20... | collective-permute-start | bytes 393224 | tf_op jit(solution)/shard_map/ppermute | solution.py:75
  98.2 4.1 %dynamic-slice_bitcast_fusion = (bf16[8,128,1024]{2,1,0:T(8,128)(2,1)S(1)}, bf16[8,128,1024]{2,1,0:T(8,128)(2,1)}) fusion(s32[]{:T(128)S(6)} %select_n.105, s32[]{:T(128)S(6)} %select_n.104, bf16[8,2,128,1280]{3,2,1,0:T(8,128)(2,1)} %bitcast.113), kind=kLoop, calls=%fused_computation | loop fusion | bytes 8388616 | tf_op jit(solution)/shard_map/reshape | solution.py:209
  102.3 0.0 collective-permute-done.1
  102.4 0.1 broadcast_in_dim.8
  102.5 14.2 %all_to_all.43.parts_ref = bf16[16,128,128]{2,1,0:T(8,128)(2,1)S(1)} all-to-all(bf16[16,128,128]{2,1,0:T(8,128)(2,1)S(1)} %bitcast.115), channel_id=1, replica_groups=mesh['z'=16,'xl'=2,'y'=4,'xh'=2,'core'=2] {'xl','y','xh'}, dimensions={0} | all-to-all | bytes 1048576 | tf_op jit(solution)/shard_map/all_to_all | solution.py:85
  116.7 10.9 %collective-permute-start.2 = (bf16[16,128,128]{2,1,0:T(8,128)(2,1)S(1)}, bf16[16,128,128]{2,1,0:T(8,128)(2,1)S(1)}, u32[]{:S(2)}, u32[]{:S(2)}) collective-permute-start(bf16[16,128,128]{2,1,0:T(8,128)(2,1)S(1)} %all_to_all.43.parts_ref), channel_id=1, source_target_pairs={{0,1},{1,0},{2,3},{3,2},{4,5},{5,4},{6,7},{7,6},{8,9},{9,8},{10,11... | collective-permute-start | bytes 1572872 | tf_op jit(solution)/shard_map/ppermute | solution.py:75
  127.6 0.0 copy-start
  127.7 1.7 %copy-done.1 = bf16[8,128,1024]{2,1,0:T(8,128)(2,1)S(1)} copy-done((bf16[8,128,1024]{2,1,0:T(8,128)(2,1)S(1)}, bf16[8,128,1024]{2,1,0:T(8,128)(2,1)}, u32[]{:S(2)}) %copy-start.1) | copy-done | bytes 2097176
  129.4 1.3 shard_map.110
  130.7 1.3 shard_map.111
  132.0 2.2 %collective-permute-start.3 = (bf16[144,1024]{1,0:T(8,128)(2,1)S(1)}, bf16[144,1024]{1,0:T(8,128)(2,1)S(1)}, u32[]{:S(2)}, u32[]{:S(2)}) collective-permute-start(bf16[144,1024]{1,0:T(8,128)(2,1)S(1)} %get-tuple-element.26), channel_id=1, source_target_pairs={{0,16},{16,0},{1,17},{17,1},{2,18},{18,2},{3,19},{19,3},{4,20},{20... | collective-permute-start | bytes 884744 | tf_op jit(solution)/shard_map/ppermute | solution.py:75
  134.2 8.3 %collective-permute-done.3.far_ref = bf16[144,1024]{1,0:T(8,128)(2,1)S(1)} collective-permute-done((bf16[144,1024]{1,0:T(8,128)(2,1)S(1)}, bf16[144,1024]{1,0:T(8,128)(2,1)S(1)}, u32[]{:S(2)}, u32[]{:S(2)}) %collective-permute-start.3) | collective-permute-done | bytes 294944 | tf_op jit(solution)/shard_map/ppermute | solution.py:75
  142.5 1.2 shard_map.112
  143.7 2.7 %collective-permute-start.4 = (bf16[8,128,256]{2,1,0:T(8,128)(2,1)S(1)}, bf16[8,128,256]{2,1,0:T(8,128)(2,1)S(1)}, u32[]{:S(2)}, u32[]{:S(2)}) collective-permute-start(bf16[8,128,256]{2,1,0:T(8,128)(2,1)S(1)} %get-tuple-element.29), channel_id=1, source_target_pairs={{0,1},{1,0},{2,3},{3,2},{4,5},{5,4},{6,7},{7,6},{8,9},{9,8},{10,11... | collective-permute-start | bytes 1572872 | tf_op jit(solution)/shard_map/ppermute | solution.py:75
  146.4 1.0 shard_map.113
  147.4 0.5 collective-permute-done.4
  147.9 0.2 add_convert_fusion
  148.1 13.5 %all_to_all.44 = bf16[8,128,256]{2,1,0:T(8,128)(2,1)S(1)} all-to-all(bf16[8,128,256]{2,1,0:T(8,128)(2,1)S(1)} %add_convert_fusion), channel_id=1, replica_groups=mesh['z'=16,'xl'=2,'y'=4,'xh'=2,'core'=2] {'y','xh'}, dimensions={0} | all-to-all | bytes 1048576 | tf_op jit(solution)/shard_map/all_to_all | solution.py:275
  161.6 0.1 convert_reduce_fusion
  161.7 0.7 copy.45
  (14 shorter events, 0.2 us)
Async XLA Ops:
  6.5 86.0 %all-gather.2.cloned.1.call-start = ((), (), s32[]{:S(2)}) async-start(), calls=%async_computation.5 | async-start | bytes 5570560 | tf_op jit(solution)/shard_map/all_gather | solution.py:203
  9.8 29.6 %all-to-all-start = ((bf16[32,8,128]{2,1,0:T(8,128)(2,1)}), bf16[32,8,128]{2,1,0:T(8,128)(2,1)S(1)}, u32[]{:S(2)}, u32[]{:S(2)}) async-start(bf16[32,8,128]{2,1,0:T(8,128)(2,1)} %fusion.23), calls=%async_computation | async-start | bytes 131072 | tf_op jit(solution)/shard_map/all_to_all | solution.py:212
  33.1 32.3 %copy-start.2 = (bf16[256,128]{1,0:T(8,128)(2,1)S(1)}, bf16[256,128]{1,0:T(8,128)(2,1)}, u32[]{:S(2)}) copy-start(bf16[256,128]{1,0:T(8,128)(2,1)} %param.11) | copy-start | bytes 196612
  40.9 45.5 %copy-start.3 = (bf16[256,128]{1,0:T(8,128)(2,1)S(1)}, bf16[256,128]{1,0:T(8,128)(2,1)}, u32[]{:S(2)}) copy-start(bf16[256,128]{1,0:T(8,128)(2,1)} %param.16) | copy-start | bytes 196612
  81.0 12.9 %collective-permute-start = (bf16[16,128,128]{2,1,0:T(8,128)(2,1)S(1)}, bf16[16,128,128]{2,1,0:T(8,128)(2,1)S(1)}, u32[]{:S(2)}, u32[]{:S(2)}) collective-permute-start(bf16[16,128,128]{2,1,0:T(8,128)(2,1)S(1)} %all_to_all.42.own_ref), channel_id=1, source_target_pairs={{0,1},{1,0},{2,3},{3,2},{4,5},{5,4},{6,7},{7,6},{8,9},{9,8},{10,11... | collective-permute-start | bytes 1572872 | tf_op jit(solution)/shard_map/ppermute | solution.py:75
  94.9 32.8 %copy-start.4 = (f32[4096]{0:T(1024)S(1)}, f32[4096]{0:T(1024)}, u32[]{:S(2)}) copy-start(f32[4096]{0:T(1024)} %param.17) | copy-start | bytes 49156
  94.9 7.4 %collective-permute-start.1 = (f32[128,256]{1,0:T(8,128)S(1)}, f32[128,256]{1,0:T(8,128)S(1)}, u32[]{:S(2)}, u32[]{:S(2)}) collective-permute-start(f32[128,256]{1,0:T(8,128)S(1)} %get-tuple-element.19), channel_id=1, source_target_pairs={{0,16},{16,0},{1,17},{17,1},{2,18},{18,2},{3,19},{19,3},{4,20},{20... | collective-permute-start | bytes 393224 | tf_op jit(solution)/shard_map/ppermute | solution.py:75
  116.7 14.0 %collective-permute-start.2 = (bf16[16,128,128]{2,1,0:T(8,128)(2,1)S(1)}, bf16[16,128,128]{2,1,0:T(8,128)(2,1)S(1)}, u32[]{:S(2)}, u32[]{:S(2)}) collective-permute-start(bf16[16,128,128]{2,1,0:T(8,128)(2,1)S(1)} %all_to_all.43.parts_ref), channel_id=1, source_target_pairs={{0,1},{1,0},{2,3},{3,2},{4,5},{5,4},{6,7},{7,6},{8,9},{9,8},{10,11... | collective-permute-start | bytes 1572872 | tf_op jit(solution)/shard_map/ppermute | solution.py:75
  127.6 14.9 %copy-start = (bf16[512,4096]{1,0:T(8,128)(2,1)S(1)}, bf16[512,4096]{1,0:T(8,128)(2,1)}, u32[]{:S(2)}) copy-start(bf16[512,4096]{1,0:T(8,128)(2,1)} %w_ref.3) | copy-start | bytes 12582916
  127.7 1.7 %copy-start.1 = (bf16[8,128,1024]{2,1,0:T(8,128)(2,1)S(1)}, bf16[8,128,1024]{2,1,0:T(8,128)(2,1)}, u32[]{:S(2)}) copy-start(bf16[8,128,1024]{2,1,0:T(8,128)(2,1)} %get-tuple-element.32.w_ref) | copy-start | bytes 6291460
  132.0 10.5 %collective-permute-start.3 = (bf16[144,1024]{1,0:T(8,128)(2,1)S(1)}, bf16[144,1024]{1,0:T(8,128)(2,1)S(1)}, u32[]{:S(2)}, u32[]{:S(2)}) collective-permute-start(bf16[144,1024]{1,0:T(8,128)(2,1)S(1)} %get-tuple-element.26), channel_id=1, source_target_pairs={{0,16},{16,0},{1,17},{17,1},{2,18},{18,2},{3,19},{19,3},{4,20},{20... | collective-permute-start | bytes 884744 | tf_op jit(solution)/shard_map/ppermute | solution.py:75
  143.7 4.2 %collective-permute-start.4 = (bf16[8,128,256]{2,1,0:T(8,128)(2,1)S(1)}, bf16[8,128,256]{2,1,0:T(8,128)(2,1)S(1)}, u32[]{:S(2)}, u32[]{:S(2)}) collective-permute-start(bf16[8,128,256]{2,1,0:T(8,128)(2,1)S(1)} %get-tuple-element.29), channel_id=1, source_target_pairs={{0,1},{1,0},{2,3},{3,2},{4,5},{5,4},{6,7},{7,6},{8,9},{9,8},{10,11... | collective-permute-start | bytes 1572872 | tf_op jit(solution)/shard_map/ppermute | solution.py:75
Sparse Core Ops, SparseCore 0:
  9.4 83.0 all-gather.1

commit v3 on v2

--- a/solution.py
+++ b/solution.py
@@ -79,42 +79,36 @@
     return lax.optimization_barrier((array,) + others)[0]
 
 
-def to_plane(tile):
-    halves = tile.reshape(128, 2, 128).transpose(1, 0, 2)[:, None]
-    spread = jnp.broadcast_to(halves, (2, 8, 128, 128)).reshape(16, 128, 128)
+def gather_plane(spread):
     return lax.all_to_all(spread, ("xl", "y", "xh"), split_axis=0, concat_axis=0, tiled=True)
 
 
-def both_tiles(parts_ref, side, index):
-    far, near = (1 - side) * 8, side * 8
-    return jnp.concatenate(
-        [
-            jnp.concatenate([parts_ref[far + index + i], parts_ref[near + index + i]], axis=0)
-            for i in range(2)
-        ],
-        axis=1,
-    )
-
-
-def mix_kernel(where_ref, own_ref, other_ref, w_own_ref, w_other_ref, far_ref, near_ref):
-    side = where_ref[1]
+def mix_kernel(
+    where_ref, own_ref, other_ref, residual_ref, w_own_ref, w_other_ref, out_ref, total_ref
+):
     total = jnp.zeros((256, 256), jnp.float32)
     for parts_ref, w_ref in ((own_ref, w_own_ref), (other_ref, w_other_ref)):
-        for i in range(4):
+        for i in range(0, 8, 2):
+            rows = [
+                jnp.concatenate([parts_ref[i + j], parts_ref[8 + i + j]], axis=0) for j in range(2)
+            ]
             total += jnp.dot(
-                both_tiles(parts_ref, side, 2 * i),
-                w_ref[2 * i : 2 * i + 2].reshape(256, 256),
+                jnp.concatenate(rows, axis=1),
+                w_ref[i : i + 2].reshape(256, 256),
                 preferred_element_type=jnp.float32,
             )
-    far_ref[...] = total[:128]
-    near_ref[...] = total[128:]
-
-
-def half_ffw(side, parts_ref, gain_ref, w_ref):
-    total = jnp.zeros((256, 1024), jnp.float32)
-    power = jnp.zeros((256, 1), jnp.float32)
+    total_ref[...] = total
+    near = pl.ds(pl.multiple_of(where_ref[1] * 128, 128), 128)
+    total_ref[near] = total_ref[near] + residual_ref[...].astype(jnp.float32)
+    out_ref[0] = total_ref[:, :128].astype(jnp.bfloat16)
+    out_ref[1] = total_ref[:, 128:].astype(jnp.bfloat16)
+
+
+def half_ffw(tokens, parts_ref, gain_ref, w_ref):
+    total, power = 0.0, 0.0
     for i in range(4):
-        wide = both_tiles(parts_ref, side, 2 * i).astype(jnp.float32)
+        wide = jnp.concatenate([parts_ref[2 * i, tokens], parts_ref[2 * i + 1, tokens]], axis=1)
+        wide = wide.astype(jnp.float32)
         power += jnp.sum(wide * wide, axis=1, keepdims=True)
         scaled = wide * gain_ref[:, i * 256 : i * 256 + 256]
         total += jnp.dot(
@@ -122,37 +116,44 @@
             w_ref[2 * i : 2 * i + 2].reshape(256, 1024),
             preferred_element_type=jnp.float32,
         )
-    return total, jnp.broadcast_to(power, (256, 128))
+    return total, jnp.broadcast_to(power, (power.shape[0], 128))
 
 
 def first_kernel(where_ref, parts_ref, gain_ref, w_ref, total_ref, power_ref):
-    total, power = half_ffw(where_ref[1], parts_ref, gain_ref, w_ref)
-    total_ref[...] = total
-    power_ref[...] = power
-
-
-def second_kernel(
-    where_ref, parts_ref, gain_ref, begun_ref, power_ref, w_ref, far_ref, near_ref, own_power_ref
-):
-    total, power = half_ffw(where_ref[1], parts_ref, gain_ref, w_ref)
-    total += begun_ref[...]
-    power += power_ref[...]
-    far_ref[:128] = total[:128].astype(jnp.bfloat16)
-    row = power[:128].T[:16]
+    total_ref[...], power_ref[...] = half_ffw(pl.ds(0, 256), parts_ref, gain_ref, w_ref)
+
+
+def far_kernel(
+    where_ref, parts_ref, gain_ref, begun_ref, power_ref, own_ref, w_ref, out_ref
+):
+    far = pl.ds(pl.multiple_of((1 - where_ref[1]) * 128, 128), 128)
+    total, power = half_ffw(far, parts_ref, gain_ref, w_ref)
+    out_ref[:128] = (total + begun_ref[far]).astype(jnp.bfloat16)
+    row = (power + power_ref[far]).T[:16]
     high = row.astype(jnp.bfloat16)
     low = (row - high.astype(jnp.float32)).astype(jnp.bfloat16)
-    pair = jnp.concatenate([high, low], axis=1)
-    far_ref[128:] = jnp.concatenate([pair, pair, pair, pair], axis=1)
-    near_ref[...] = total[128:]
-    own_power_ref[...] = power[128:]
+    out_ref[128:144] = jnp.concatenate([high, low] * 4, axis=1)
+    stream = own_ref[where_ref[2], far]
+    out_ref[144:] = jnp.concatenate([stream[16 * i : 16 * i + 16] for i in range(8)], axis=1)
+
+
+def near_kernel(
+    where_ref, parts_ref, gain_ref, begun_ref, power_ref, w_ref, total_ref, own_power_ref
+):
+    near = pl.ds(pl.multiple_of(where_ref[1] * 128, 128), 128)
+    total, power = half_ffw(near, parts_ref, gain_ref, w_ref)
+    total_ref[...] = total + begun_ref[near]
+    own_power_ref[...] = power + power_ref[near]
 
 
 def columns_of(w_ref, index, core):
     return w_ref[:, pl.ds(pl.multiple_of((2 * index + core) * 256, 256), 256)]
 
 
-def down_far_kernel(where_ref, near_ref, far_ref, power_ref, w_ref, out_ref, hidden_ref):
-    sums = far_ref[128:].astype(jnp.float32)
+def down_far_kernel(
+    where_ref, near_ref, far_ref, power_ref, own_ref, w_ref, out_ref, hidden_ref, stream_ref
+):
+    sums = far_ref[128:144].astype(jnp.float32)
     sums = jnp.broadcast_to(sums[:1, :128] + sums[:1, 128:256], (128, 128)).T
     inverse_rms = lax.rsqrt((power_ref[:, :1] + sums[:, :1]) / 4096 + EPSILON)
     both = (near_ref[...] + far_ref[:128].astype(jnp.float32)) * inverse_rms
@@ -162,6 +163,12 @@
         out_ref[i] = jnp.dot(
             hidden, columns_of(w_ref, i, 1 - where_ref[0]), preferred_element_type=jnp.float32
         ).astype(jnp.bfloat16)
+    side = where_ref[1]
+    packed = far_ref[144:]
+    back = jnp.concatenate([packed[:, 128 * i : 128 * i + 128] for i in range(8)], axis=0)
+    kept = own_ref[where_ref[2], pl.ds(pl.multiple_of(side * 128, 128), 128)]
+    stream_ref[:, :128] = jnp.where(side == 0, kept, back)
+    stream_ref[:, 128:] = jnp.where(side == 0, back, kept)
 
 
 def down_near_kernel(where_ref, hidden_ref, w_ref, out_ref):
@@ -171,7 +178,7 @@
         )
 
 
-def local_call(kernel, where, operands, outs, flops):
+def local_call(kernel, where, operands, outs, flops, scratch=()):
     outs = [jax.ShapeDtypeStruct(shape, dtype) for shape, dtype in outs]
     return pl.pallas_call(
         kernel,
@@ -179,6 +186,7 @@
         + [pl.BlockSpec(memory_space=pltpu.VMEM)] * len(operands),
         out_specs=[pl.BlockSpec(memory_space=pltpu.VMEM)] * len(outs),
         out_shape=outs,
+        scratch_shapes=scratch,
         compiler_params=pltpu.CompilerParams(vmem_limit_bytes=16 * 1024 * 1024),
         cost_estimate=pl.CostEstimate(flops=flops, bytes_accessed=2**21, transcendentals=0),
     )(where, *operands)
@@ -199,7 +207,8 @@
 ):
     side = lax.axis_index("xl")
     core = lax.axis_index("core")
-    where = jnp.stack([core, side]).astype(jnp.int32)
+    column = lax.axis_index(("y", "xh"))
+    where = jnp.stack([core, side, column]).astype(jnp.int32)
     weights = lax.all_gather(
         jnp.concatenate([w_gate, w_up, w_out], axis=1), "z", axis=0, tiled=True
     ).reshape(8, 2, 128, 1280)
@@ -220,21 +229,29 @@
     convolved = inverse_dft(joint_re, joint_im, tables, length).astype(jnp.bfloat16)
     convolved = lax.all_to_all(convolved, ROW, split_axis=1, concat_axis=0, tiled=True)
     gated = (q_stream.astype(jnp.float32) * convolved.astype(jnp.float32)).astype(jnp.bfloat16)
-    own = to_plane(gated.T)
+    halves = gated.T.reshape(128, 2, 128).transpose(1, 0, 2)[:, None]
+    own = gather_plane(jnp.broadcast_to(halves, (2, 8, 128, 128)).reshape(16, 128, 128))
     other = swap(own, "core")
-    far, near = local_call(
+    mixed = local_call(
         mix_kernel,
         where,
-        (own, other, rows_of(weights, core, 1024, 256), rows_of(weights, 1 - core, 1024, 256)),
-        [((128, 256), jnp.float32)] * 2,
+        (
+            own,
+            other,
+            residual.T,
+            rows_of(weights, core, 1024, 256),
+            rows_of(weights, 1 - core, 1024, 256),
+        ),
+        [((2, 256, 128), jnp.bfloat16)],
         2 * 256 * 256 * 2048,
-    )
-    weights = after(weights, near)
+        [pltpu.VMEM((256, 256), jnp.float32)],
+    )[0]
+    spread = jnp.broadcast_to(mixed[:, None], (2, 8, 256, 128)).reshape(16, 256, 128)
+    pairs = gather_plane(spread)
+    weights = after(weights, pairs)
+    pairs = pairs.reshape(2, 8, 256, 128)
+    own = (pairs[0].astype(jnp.float32) + pairs[1].astype(jnp.float32)).astype(jnp.bfloat16)
     w_own, w_other = rows_of(weights, core, 0, 1024), rows_of(weights, 1 - core, 0, 1024)
-    far = swap(far, "xl")
-    far = after(far, w_own, w_other)
-    stream = (residual.T.astype(jnp.float32) + (near + far)).astype(jnp.bfloat16)
-    own = to_plane(stream)
     other = swap(own, "core")
     gains = lax.dynamic_index_in_dim(norm_gain.reshape(8, 2, 2, 128), side, 2, keepdims=False)
     gain_own = lax.dynamic_index_in_dim(gains, core, 1, keepdims=False).reshape(1, 1024)
@@ -247,19 +264,27 @@
         2 * 256 * 1024 * 1024,
     )
     other = after(other, begun)
-    far, near, power = local_call(
-        second_kernel,
+    far = local_call(
+        far_kernel,
+        where,
+        (other, gain_other, begun, power, own, w_other),
+        [((160, 1024), jnp.bfloat16)],
+        2 * 128 * 1024 * 1024,
+    )[0]
+    near, power = local_call(
+        near_kernel,
         where,
         (other, gain_other, begun, power, w_other),
-        [((144, 1024), jnp.bfloat16), ((128, 1024), jnp.float32), ((128, 128), jnp.float32)],
-        2 * 256 * 1024 * 1024,
+        [((128, 1024), jnp.float32), ((128, 128), jnp.float32)],
+        2 * 128 * 1024 * 1024,
     )
     far = swap(far, "xl")
-    far, hidden = local_call(
+    far = after(far, near)
+    far, hidden, stream = local_call(
         down_far_kernel,
         where,
-        (near, far, power, w_down),
-        [((8, 128, 256), jnp.bfloat16), ((128, 512), jnp.bfloat16)],
+        (near, far, power, own, w_down),
+        [((8, 128, 256), jnp.bfloat16), ((128, 512), jnp.bfloat16), ((128, 256), jnp.bfloat16)],
         2 * 128 * 512 * 2048,
     )
     far = swap(far, "core")

time: 170 us -> 169 us (level)
  blocking collectives: 62.3 us -> 48.9 us
  waiting for transfers between devices: 21.2 us -> 31.5 us
  starting transfers between devices: 41.5 us -> 44.4 us
  local copies, waits for them, and re-layouts: 10.3 us -> 8.24 us
    all_to_all x2 -> x1, blocking collectives: 29.5 us -> 15.4 us  [gather_plane(): lax.all_to_all(spread, ('xl', 'y', 'xh'), split_axis=0, concat_axis=0, ti...]
    all_to_all x0 -> x1, waiting for transfers between devices: none -> 11 us  [gather_plane(): lax.all_to_all(spread, ('xl', 'y', 'xh'), split_axis=0, concat_axis=0, ti...]
    all_to_all x0 -> x1, starting transfers between devices: none -> 6.8 us  [gather_plane(): lax.all_to_all(spread, ('xl', 'y', 'xh'), split_axis=0, concat_axis=0, ti...]
    ppermute x5 -> x4, starting transfers between devices: 24.5 us -> 20.6 us  [swap(): return lax.ppermute(array, axis, [(0, 1), (1, 0)])]
    unnamed x12 -> x10, local copies, waits for them, and re-layouts: 1.95 us -> 0.22 us
    pallas_call x5 -> x6, Pallas kernels: 5.66 us -> 6.46 us  [local_call(): pl.pallas_call(kernel, in_specs=[pl.BlockSpec(memory_space=pltpu.SMEM)] +...]
    ppermute x5 -> x4, waiting for transfers between devices: 8.83 us -> 8.28 us  [swap(): return lax.ppermute(array, axis, [(0, 1), (1, 0)])]
  transfers between devices with their start and end apart: 7 -> 7, of which waited for: 4 -> 5; matrix products, arithmetic and copies ran while one was open for 12% -> 11% of each run, Pallas kernels for 1% -> 2%
where the time goes in v3:
time: 169 us; the launch traced here: 168 us
  blocking collectives  48.9 us (29%)
  starting transfers between devices  44.4 us (26%)
  waiting for transfers between devices  31.5 us (19%)
  between operations  13.8 us (8%)
  matrix products  9.99 us (6%)
  local copies, waits for them, and re-layouts  8.24 us (5%)
  Pallas kernels  6.46 us (4%)
  other arithmetic  4.64 us (3%)
    ppermute x4, starting transfers between devices, swap(): return lax.ppermute(array, axis, [(0, 1), (1, 0)])  20.6 us
    all_to_all x1, blocking collectives, on_device(): lax.all_to_all(convolved, ROW, split_axis=1, concat_axis=0, tiled=True)  19.2 us
    all_to_all x1, starting transfers between devices, on_device(): lax.all_to_all(product, ROW, split_axis=0, concat_axis=1, tiled=True)  17 us
    all_to_all x1, blocking collectives, gather_plane(): lax.all_to_all(spread, ('xl', 'y', 'xh'), split_axis=0, concat_axis=0, ti...  15.4 us
    all_to_all x1, blocking collectives, on_device(): lax.all_to_all(down, ('y', 'xh'), split_axis=0, concat_axis=0, tiled=True)  14.3 us
    all_to_all x1, waiting for transfers between devices, gather_plane(): lax.all_to_all(spread, ('xl', 'y', 'xh'), split_axis=0, concat_axis=0, ti...  11 us
    ppermute x4, waiting for transfers between devices, swap(): return lax.ppermute(array, axis, [(0, 1), (1, 0)])  8.28 us
    dot_general x12, matrix products, apply_last(): jnp.einsum('ckn,nm->ckm', blocks, matrix, precision=lax.Precision.HIGHEST)  7.41 us
  transfers between devices with their start and end apart: 7, of which 5 were waited for; matrix products, arithmetic and copies ran while one was open for 11% of the time, Pallas kernels for 2%

profile of v3, /device:TPU:1, one launch (start us, length us, event | category | flops | bytes accessed | tf_op | source)
XLA Modules:
  0.0 167.9 jit_solution(13380993090311546496)
XLA Ops:
  6.5 1.8 %pad_maximum_fusion = bf16[128,1280]{1,0:T(8,128)(2,1)} fusion(bf16[128,256]{1,0:T(8,128)(2,1)} %param.18, bf16[128,512]{1,0:T(8,128)(2,1)} %param.20, bf16[128,512]{1,0:T(8,128)(2,1)} %param.19), kind=kLoop, calls=%fused_computation.21 | loop fusion | flops 983040 | bytes 655360 | tf_op jit(solution)/shard_map/concatenate | solution.py:213
  8.3 0.0 all-gather.2.cloned.1.call-update
  8.3 1.5 fusion.22
  9.9 17.0 %all-to-all-start = ((bf16[32,8,128]{2,1,0:T(8,128)(2,1)}), bf16[32,8,128]{2,1,0:T(8,128)(2,1)S(1)}, u32[]{:S(2)}, u32[]{:S(2)}) async-start(bf16[32,8,128]{2,1,0:T(8,128)(2,1)} %fusion.22), calls=%async_computation | async-start | bytes 131072 | tf_op jit(solution)/shard_map/all_to_all | solution.py:221
  26.8 1.0 slice.15
  27.8 0.7 slice.14
  28.5 0.1 copy.43
  28.6 0.7 bitcast_add_fusion
  29.3 0.1 copy.34
  29.3 0.1 sine_negate_fusion.7
  29.5 0.1 maximum_bitcast_fusion
  29.6 0.5 convolution_bitcast_fusion
  30.1 0.5 convolution_bitcast_fusion.1
  30.6 0.6 fusion.38
  31.2 0.6 convolution_subtract_fusion.1
  31.8 0.6 fusion.26
  32.5 0.6 convolution_add_fusion.1
  33.1 0.0 copy-start.1
  33.1 6.4 %all-to-all-done = bf16[32,8,128]{2,1,0:T(8,128)(2,1)S(1)} async-done(((bf16[32,8,128]{2,1,0:T(8,128)(2,1)}), bf16[32,8,128]{2,1,0:T(8,128)(2,1)S(1)}, u32[]{:S(2)}, u32[]{:S(2)}) %all-to-all-start) | async-done | bytes 65568 | tf_op jit(solution)/shard_map/all_to_all | solution.py:221
  39.5 0.4 convolution_bitcast_fusion.2
  39.9 0.4 convolution_bitcast_fusion.3
  40.3 0.6 fusion.40
  40.9 0.0 copy-start.2
  40.9 0.6 fusion.28
  41.5 0.6 convolution_subtract_fusion.2
  42.1 0.7 multiply_subtract_fusion
  42.8 0.6 fusion.34
  43.4 0.6 fusion.32
  44.0 0.6 convolution_add_fusion
  44.7 0.6 convolution_subtract_fusion
  45.3 0.4 fusion.6
  45.7 0.4 fusion.2
  46.1 19.2 %all_to_all.41 = bf16[8,32,128]{2,0,1:T(8,128)(2,1)S(1)} all-to-all(bf16[8,32,128]{2,0,1:T(8,128)(2,1)S(1)} %copy.35), channel_id=1, replica_groups=mesh['z'=16,'xl'=2,'y'=4,'xh'=2,'core'=2] {'z','xl'}, dimensions={1} | all-to-all | bytes 131072 | tf_op jit(solution)/shard_map/all_to_all | solution.py:230
  65.3 0.1 copy.36
  65.5 0.1 broadcast_in_dim.7
  65.6 0.0 copy-start.3
  65.6 15.4 %all_to_all.42.own_ref = bf16[16,128,128]{2,1,0:T(8,128)(2,1)S(1)} all-to-all(bf16[16,128,128]{2,1,0:T(8,128)(2,1)S(1)} %bitcast.112), channel_id=1, replica_groups=mesh['z'=16,'xl'=2,'y'=4,'xh'=2,'core'=2] {'xl','y','xh'}, dimensions={0} | all-to-all | bytes 1048576 | tf_op jit(solution)/shard_map/all_to_all | solution.py:83
  81.0 5.4 %collective-permute-start = (bf16[16,128,128]{2,1,0:T(8,128)(2,1)S(1)}, bf16[16,128,128]{2,1,0:T(8,128)(2,1)S(1)}, u32[]{:S(2)}, u32[]{:S(2)}) collective-permute-start(bf16[16,128,128]{2,1,0:T(8,128)(2,1)S(1)} %all_to_all.42.own_ref), channel_id=1, source_target_pairs={{0,1},{1,0},{2,3},{3,2},{4,5},{5,4},{6,7},{7,6},{8,9},{9,8},{10,11... | collective-permute-start | bytes 1572872 | tf_op jit(solution)/shard_map/ppermute | solution.py:75
  86.4 0.1 copy.37
  86.5 0.1 pad_add_fusion.where_ref
  86.6 5.9 %all-gather.2.cloned.1.call-done = bf16[2048,1280]{1,0:T(8,128)(2,1)} async-done(((bf16[128,1280]{1,0:T(8,128)(2,1)}), bf16[2048,1280]{1,0:T(8,128)(2,1)}) %all-gather.2.cloned.1.call-update) | async-done | bytes 5242896 | tf_op jit(solution)/shard_map/all_gather | solution.py:212
  92.5 1.3 dynamic-slice_bitcast_fusion.2
  93.8 0.0 collective-permute-done.other_ref
  93.8 1.0 shard_map.109
  94.9 1.2 broadcast_in_dim.8
  96.1 6.8 %all-to-all-start.3 = ((bf16[16,256,128]{2,1,0:T(8,128)(2,1)}), bf16[16,256,128]{2,1,0:T(8,128)(2,1)S(1)}, u32[]{:S(2)}, u32[]{:S(2)}) async-start(bf16[16,256,128]{2,1,0:T(8,128)(2,1)} %bitcast.25), calls=%async_computation.3 | async-start | bytes 2097152 | tf_op jit(solution)/shard_map/all_to_all | solution.py:83
  102.9 11.0 %all-to-all-done.3 = bf16[16,256,128]{2,1,0:T(8,128)(2,1)S(1)} async-done(((bf16[16,256,128]{2,1,0:T(8,128)(2,1)}), bf16[16,256,128]{2,1,0:T(8,128)(2,1)S(1)}, u32[]{:S(2)}, u32[]{:S(2)}) %all-to-all-start.3) | async-done | bytes 1048608 | tf_op jit(solution)/shard_map/all_to_all | solution.py:83
  113.9 0.1 add_convert_fusion.1.parts_ref.own_ref
  114.0 10.1 %collective-permute-start.1 = (bf16[8,256,128]{2,1,0:T(8,128)(2,1)S(1)}, bf16[8,256,128]{2,1,0:T(8,128)(2,1)S(1)}, u32[]{:S(2)}, u32[]{:S(2)}) collective-permute-start(bf16[8,256,128]{2,1,0:T(8,128)(2,1)S(1)} %add_convert_fusion.1.parts_ref.own_ref), channel_id=1, source_target_pairs={{0,1},{1,0},{2,3},{3,2},{4,5},{5,4},{6,7},{7,6},{8,9},{9,8},{10,11... | collective-permute-start | bytes 1572872 | tf_op jit(solution)/shard_map/ppermute | solution.py:75
  124.2 2.7 %dynamic-slice_bitcast_fusion = (bf16[8,128,1024]{2,1,0:T(8,128)(2,1)S(1)}, bf16[8,128,1024]{2,1,0:T(8,128)(2,1)S(1)}) fusion(s32[]{:T(128)S(6)} %select_n.105, s32[]{:T(128)S(6)} %select_n.104, bf16[8,2,128,1280]{3,2,1,0:T(8,128)(2,1)} %bitcast.111), kind=kLoop, calls=%fused_computation | loop fusion | bytes 8388616 | tf_op jit(solution)/shard_map/reshape | solution.py:218
  126.9 0.0 copy-start
  126.9 1.3 shard_map.110
  128.2 1.0 shard_map.112
  129.2 2.4 %collective-permute-start.2 = (bf16[160,1024]{1,0:T(8,128)(2,1)S(1)}, bf16[160,1024]{1,0:T(8,128)(2,1)S(1)}, u32[]{:S(2)}, u32[]{:S(2)}) collective-permute-start(bf16[160,1024]{1,0:T(8,128)(2,1)S(1)} %shard_map.112), channel_id=1, source_target_pairs={{0,16},{16,0},{1,17},{17,1},{2,18},{18,2},{3,19},{19,3},{4,20},{20... | collective-permute-start | bytes 983048 | tf_op jit(solution)/shard_map/ppermute | solution.py:75
  131.6 1.0 shard_map.111
  132.6 7.8 %collective-permute-done.2.far_ref = bf16[160,1024]{1,0:T(8,128)(2,1)S(1)} collective-permute-done((bf16[160,1024]{1,0:T(8,128)(2,1)S(1)}, bf16[160,1024]{1,0:T(8,128)(2,1)S(1)}, u32[]{:S(2)}, u32[]{:S(2)}) %collective-permute-start.2) | collective-permute-done | bytes 327712 | tf_op jit(solution)/shard_map/ppermute | solution.py:75
  140.4 1.2 shard_map.113
  141.6 2.7 %collective-permute-start.3 = (bf16[8,128,256]{2,1,0:T(8,128)(2,1)S(1)}, bf16[8,128,256]{2,1,0:T(8,128)(2,1)S(1)}, u32[]{:S(2)}, u32[]{:S(2)}) collective-permute-start(bf16[8,128,256]{2,1,0:T(8,128)(2,1)S(1)} %get-tuple-element.25), channel_id=1, source_target_pairs={{0,1},{1,0},{2,3},{3,2},{4,5},{5,4},{6,7},{7,6},{8,9},{9,8},{10,11... | collective-permute-start | bytes 1572872 | tf_op jit(solution)/shard_map/ppermute | solution.py:75
  144.3 1.0 shard_map.114
  145.4 0.5 collective-permute-done.3
  145.8 0.1 add_convert_fusion
  146.0 14.3 %all_to_all.43 = bf16[8,128,256]{2,1,0:T(8,128)(2,1)S(1)} all-to-all(bf16[8,128,256]{2,1,0:T(8,128)(2,1)S(1)} %add_convert_fusion), channel_id=1, replica_groups=mesh['z'=16,'xl'=2,'y'=4,'xh'=2,'core'=2] {'y','xh'}, dimensions={0} | all-to-all | bytes 1048576 | tf_op jit(solution)/shard_map/all_to_all | solution.py:300
  160.3 0.1 convert_reduce_fusion
  160.4 0.7 copy.42
  (10 shorter events, 0.1 us)
Async XLA Ops:
  6.5 86.0 %all-gather.2.cloned.1.call-start = ((), (), s32[]{:S(2)}) async-start(), calls=%async_computation.5 | async-start | bytes 5570560 | tf_op jit(solution)/shard_map/all_gather | solution.py:212
  9.9 29.6 %all-to-all-start = ((bf16[32,8,128]{2,1,0:T(8,128)(2,1)}), bf16[32,8,128]{2,1,0:T(8,128)(2,1)S(1)}, u32[]{:S(2)}, u32[]{:S(2)}) async-start(bf16[32,8,128]{2,1,0:T(8,128)(2,1)} %fusion.22), calls=%async_computation | async-start | bytes 131072 | tf_op jit(solution)/shard_map/all_to_all | solution.py:221
  33.1 32.2 %copy-start.1 = (bf16[256,128]{1,0:T(8,128)(2,1)S(1)}, bf16[256,128]{1,0:T(8,128)(2,1)}, u32[]{:S(2)}) copy-start(bf16[256,128]{1,0:T(8,128)(2,1)} %param.11) | copy-start | bytes 196612
  40.9 45.5 %copy-start.2 = (bf16[256,128]{1,0:T(8,128)(2,1)S(1)}, bf16[256,128]{1,0:T(8,128)(2,1)}, u32[]{:S(2)}) copy-start(bf16[256,128]{1,0:T(8,128)(2,1)} %param.16) | copy-start | bytes 196612
  65.6 58.6 %copy-start.3 = (f32[4096]{0:T(1024)S(1)}, f32[4096]{0:T(1024)}, u32[]{:S(2)}) copy-start(f32[4096]{0:T(1024)} %param.17) | copy-start | bytes 49156
  81.0 12.8 %collective-permute-start = (bf16[16,128,128]{2,1,0:T(8,128)(2,1)S(1)}, bf16[16,128,128]{2,1,0:T(8,128)(2,1)S(1)}, u32[]{:S(2)}, u32[]{:S(2)}) collective-permute-start(bf16[16,128,128]{2,1,0:T(8,128)(2,1)S(1)} %all_to_all.42.own_ref), channel_id=1, source_target_pairs={{0,1},{1,0},{2,3},{3,2},{4,5},{5,4},{6,7},{7,6},{8,9},{9,8},{10,11... | collective-permute-start | bytes 1572872 | tf_op jit(solution)/shard_map/ppermute | solution.py:75
  96.1 17.8 %all-to-all-start.3 = ((bf16[16,256,128]{2,1,0:T(8,128)(2,1)}), bf16[16,256,128]{2,1,0:T(8,128)(2,1)S(1)}, u32[]{:S(2)}, u32[]{:S(2)}) async-start(bf16[16,256,128]{2,1,0:T(8,128)(2,1)} %bitcast.25), calls=%async_computation.3 | async-start | bytes 2097152 | tf_op jit(solution)/shard_map/all_to_all | solution.py:83
  114.0 14.2 %collective-permute-start.1 = (bf16[8,256,128]{2,1,0:T(8,128)(2,1)S(1)}, bf16[8,256,128]{2,1,0:T(8,128)(2,1)S(1)}, u32[]{:S(2)}, u32[]{:S(2)}) collective-permute-start(bf16[8,256,128]{2,1,0:T(8,128)(2,1)S(1)} %add_convert_fusion.1.parts_ref.own_ref), channel_id=1, source_target_pairs={{0,1},{1,0},{2,3},{3,2},{4,5},{5,4},{6,7},{7,6},{8,9},{9,8},{10,11... | collective-permute-start | bytes 1572872 | tf_op jit(solution)/shard_map/ppermute | solution.py:75
  126.9 13.5 %copy-start = (bf16[512,4096]{1,0:T(8,128)(2,1)S(1)}, bf16[512,4096]{1,0:T(8,128)(2,1)}, u32[]{:S(2)}) copy-start(bf16[512,4096]{1,0:T(8,128)(2,1)} %w_ref.3) | copy-start | bytes 12582916
  129.2 11.2 %collective-permute-start.2 = (bf16[160,1024]{1,0:T(8,128)(2,1)S(1)}, bf16[160,1024]{1,0:T(8,128)(2,1)S(1)}, u32[]{:S(2)}, u32[]{:S(2)}) collective-permute-start(bf16[160,1024]{1,0:T(8,128)(2,1)S(1)} %shard_map.112), channel_id=1, source_target_pairs={{0,16},{16,0},{1,17},{17,1},{2,18},{18,2},{3,19},{19,3},{4,20},{20... | collective-permute-start | bytes 983048 | tf_op jit(solution)/shard_map/ppermute | solution.py:75
  141.6 4.2 %collective-permute-start.3 = (bf16[8,128,256]{2,1,0:T(8,128)(2,1)S(1)}, bf16[8,128,256]{2,1,0:T(8,128)(2,1)S(1)}, u32[]{:S(2)}, u32[]{:S(2)}) collective-permute-start(bf16[8,128,256]{2,1,0:T(8,128)(2,1)S(1)} %get-tuple-element.25), channel_id=1, source_target_pairs={{0,1},{1,0},{2,3},{3,2},{4,5},{5,4},{6,7},{7,6},{8,9},{9,8},{10,11... | collective-permute-start | bytes 1572872 | tf_op jit(solution)/shard_map/ppermute | solution.py:75
Sparse Core Ops, SparseCore 0:
  9.4 83.0 all-gather.1

commit v4 on v3

--- a/solution.py
+++ b/solution.py
@@ -178,6 +178,14 @@
         )
 
 
+def finish_kernel(where_ref, parts_ref, stream_ref, out_ref):
+    total = parts_ref[0].astype(jnp.float32)
+    for i in range(1, 8):
+        total += parts_ref[i].astype(jnp.float32)
+    total += stream_ref[...].astype(jnp.float32)
+    out_ref[...] = total.T.astype(jnp.bfloat16)
+
+
 def local_call(kernel, where, operands, outs, flops, scratch=()):
     outs = [jax.ShapeDtypeStruct(shape, dtype) for shape, dtype in outs]
     return pl.pallas_call(
@@ -229,6 +237,10 @@
     convolved = inverse_dft(joint_re, joint_im, tables, length).astype(jnp.bfloat16)
     convolved = lax.all_to_all(convolved, ROW, split_axis=1, concat_axis=0, tiled=True)
     gated = (q_stream.astype(jnp.float32) * convolved.astype(jnp.float32)).astype(jnp.bfloat16)
+    gains = lax.dynamic_index_in_dim(norm_gain.reshape(8, 2, 2, 128), side, 2, keepdims=False)
+    gain_own = lax.dynamic_index_in_dim(gains, core, 1, keepdims=False).reshape(1, 1024)
+    gain_other = lax.dynamic_index_in_dim(gains, 1 - core, 1, keepdims=False).reshape(1, 1024)
+    gated, gain_own, gain_other = lax.optimization_barrier((gated, gain_own, gain_other))
     halves = gated.T.reshape(128, 2, 128).transpose(1, 0, 2)[:, None]
     own = gather_plane(jnp.broadcast_to(halves, (2, 8, 128, 128)).reshape(16, 128, 128))
     other = swap(own, "core")
@@ -253,9 +265,6 @@
     own = (pairs[0].astype(jnp.float32) + pairs[1].astype(jnp.float32)).astype(jnp.bfloat16)
     w_own, w_other = rows_of(weights, core, 0, 1024), rows_of(weights, 1 - core, 0, 1024)
     other = swap(own, "core")
-    gains = lax.dynamic_index_in_dim(norm_gain.reshape(8, 2, 2, 128), side, 2, keepdims=False)
-    gain_own = lax.dynamic_index_in_dim(gains, core, 1, keepdims=False).reshape(1, 1024)
-    gain_other = lax.dynamic_index_in_dim(gains, 1 - core, 1, keepdims=False).reshape(1, 1024)
     begun, power = local_call(
         first_kernel,
         where,
@@ -304,8 +313,9 @@
         concat_axis=0,
         tiled=True,
     )
-    down_out = jnp.sum(parts.astype(jnp.float32), axis=0)
-    return (stream.astype(jnp.float32) + down_out).astype(jnp.bfloat16).T
+    return local_call(
+        finish_kernel, where, (parts, stream), [((256, 128), jnp.bfloat16)], 9 * 128 * 256
+    )[0]
 
 
 def solution(mesh):

time: 169 us -> 165 us (0.976)
  local copies, waits for them, and re-layouts: 8.24 us -> 5.09 us
  blocking collectives: 48.9 us -> 46.5 us
    all_to_all x1 -> x0, blocking collectives: 19.2 us -> none  [on_device(): lax.all_to_all(convolved, ROW, split_axis=1, concat_axis=0, tiled=True)]
    all_to_all x1 -> x2, blocking collectives: 15.4 us -> 33 us  [gather_plane(): lax.all_to_all(spread, ('xl', 'y', 'xh'), split_axis=0, concat_axis=0, ti...]
    reshape x2, local copies, waits for them, and re-layouts: 4.04 us -> 2.01 us  [rows_of(): return part.reshape(8, 128, width)]
    all_to_all x1, waiting for transfers between devices: 11 us -> 12.7 us  [on_device(): lax.all_to_all(convolved, ROW, split_axis=1, concat_axis=0, tiled=True)]
    pallas_call x6 -> x7, Pallas kernels: 6.46 us -> 7.8 us  [local_call(): pl.pallas_call(kernel, in_specs=[pl.BlockSpec(memory_space=pltpu.SMEM)] +...]
where the time goes in v4:
time: 165 us; the launch traced here: 164 us
  blocking collectives  46.5 us (28%)
  starting transfers between devices  44.1 us (27%)
  waiting for transfers between devices  32.7 us (20%)
  between operations  13.8 us (8%)
  matrix products  10 us (6%)
  Pallas kernels  7.8 us (5%)
  local copies, waits for them, and re-layouts  5.09 us (3%)
  other arithmetic  4.54 us (3%)
    all_to_all x2, blocking collectives, gather_plane(): lax.all_to_all(spread, ('xl', 'y', 'xh'), split_axis=0, concat_axis=0, ti...  33 us
    ppermute x4, starting transfers between devices, swap(): return lax.ppermute(array, axis, [(0, 1), (1, 0)])  20.9 us
    all_to_all x1, starting transfers between devices, on_device(): lax.all_to_all(product, ROW, split_axis=0, concat_axis=1, tiled=True)  17 us
    all_to_all x1, blocking collectives, on_device(): lax.all_to_all(down, ('y', 'xh'), split_axis=0, concat_axis=0, tiled=True)  13.5 us
    all_to_all x1, waiting for transfers between devices, on_device(): lax.all_to_all(convolved, ROW, split_axis=1, concat_axis=0, tiled=True)  12.7 us
    ppermute x4, waiting for transfers between devices, swap(): return lax.ppermute(array, axis, [(0, 1), (1, 0)])  8.45 us
    pallas_call x7, Pallas kernels, local_call(): pl.pallas_call(kernel, in_specs=[pl.BlockSpec(memory_space=pltpu.SMEM)] +...  7.8 us
    dot_general x12, matrix products, apply_last(): jnp.einsum('ckn,nm->ckm', blocks, matrix, precision=lax.Precision.HIGHEST)  7.43 us
  transfers between devices with their start and end apart: 7, of which 5 were waited for; matrix products, arithmetic and copies ran while one was open for 11% of the time, Pallas kernels for 2%

profile of v4, /device:TPU:1, one launch (start us, length us, event | category | flops | bytes accessed | tf_op | source)
XLA Modules:
  0.0 164.5 jit_solution(4866640387928106355)
XLA Ops:
  6.5 1.8 %pad_maximum_fusion = bf16[128,1280]{1,0:T(8,128)(2,1)} fusion(bf16[128,256]{1,0:T(8,128)(2,1)} %param.18, bf16[128,512]{1,0:T(8,128)(2,1)} %param.20, bf16[128,512]{1,0:T(8,128)(2,1)} %param.19), kind=kLoop, calls=%fused_computation.20 | loop fusion | flops 983040 | bytes 655360 | tf_op jit(solution)/shard_map/concatenate | solution.py:221
  8.3 0.0 all-gather.2.cloned.1.call-update
  8.3 1.5 fusion.22
  9.8 17.0 %all-to-all-start = ((bf16[32,8,128]{2,1,0:T(8,128)(2,1)}), bf16[32,8,128]{2,1,0:T(8,128)(2,1)S(1)}, u32[]{:S(2)}, u32[]{:S(2)}) async-start(bf16[32,8,128]{2,1,0:T(8,128)(2,1)} %fusion.22), calls=%async_computation | async-start | bytes 131072 | tf_op jit(solution)/shard_map/all_to_all | solution.py:229
  26.8 0.7 slice.14
  27.5 1.0 slice.15
  28.5 0.1 copy.40
  28.6 0.7 bitcast_add_fusion
  29.2 0.1 copy.32
  29.3 0.1 sine_negate_fusion.7
  29.5 0.1 maximum_bitcast_fusion
  29.6 0.5 convolution_bitcast_fusion
  30.1 0.5 convolution_bitcast_fusion.1
  30.6 0.6 fusion.25
  31.2 0.6 convolution_add_fusion.1
  31.8 0.6 fusion.37
  32.4 0.6 convolution_subtract_fusion.1
  33.1 0.0 copy-start.4
  33.1 0.0 copy-start.2
  33.1 6.4 %all-to-all-done = bf16[32,8,128]{2,1,0:T(8,128)(2,1)S(1)} async-done(((bf16[32,8,128]{2,1,0:T(8,128)(2,1)}), bf16[32,8,128]{2,1,0:T(8,128)(2,1)S(1)}, u32[]{:S(2)}, u32[]{:S(2)}) %all-to-all-start) | async-done | bytes 65568 | tf_op jit(solution)/shard_map/all_to_all | solution.py:229
  39.5 0.4 convolution_bitcast_fusion.2
  39.9 0.4 convolution_bitcast_fusion.3
  40.3 0.6 fusion.27
  40.9 0.0 copy-start.3
  40.9 0.6 fusion.39
  41.5 0.6 convolution_subtract_fusion.2
  42.1 0.7 multiply_subtract_fusion
  42.8 0.6 fusion.33
  43.4 0.6 fusion.31
  44.0 0.6 convolution_add_fusion
  44.7 0.6 convolution_subtract_fusion
  45.3 0.4 fusion.6
  45.7 0.4 fusion.2
  46.1 0.7 copy.33
  46.8 6.2 %all-to-all-start.1 = ((bf16[8,32,128]{2,0,1:T(8,128)(2,1)}), bf16[8,32,128]{2,0,1:T(8,128)(2,1)S(1)}, u32[]{:S(2)}, u32[]{:S(2)}) async-start(bf16[8,32,128]{2,0,1:T(8,128)(2,1)} %copy.33), calls=%async_computation.1 | async-start | bytes 131072 | tf_op jit(solution)/shard_map/all_to_all | solution.py:238
  53.0 12.7 %all-to-all-done.1 = bf16[8,32,128]{2,0,1:T(8,128)(2,1)S(1)} async-done(((bf16[8,32,128]{2,0,1:T(8,128)(2,1)}), bf16[8,32,128]{2,0,1:T(8,128)(2,1)S(1)}, u32[]{:S(2)}, u32[]{:S(2)}) %all-to-all-start.1) | async-done | bytes 65568 | tf_op jit(solution)/shard_map/all_to_all | solution.py:238
  65.8 0.1 copy.34
  65.9 0.1 broadcast_in_dim.7
  66.0 15.3 %all_to_all.41.own_ref = bf16[16,128,128]{2,1,0:T(8,128)(2,1)S(1)} all-to-all(bf16[16,128,128]{2,1,0:T(8,128)(2,1)S(1)} %bitcast.111), channel_id=1, replica_groups=mesh['z'=16,'xl'=2,'y'=4,'xh'=2,'core'=2] {'xl','y','xh'}, dimensions={0} | all-to-all | bytes 1048576 | tf_op jit(solution)/shard_map/all_to_all | solution.py:83
  81.3 5.9 %collective-permute-start = (bf16[16,128,128]{2,1,0:T(8,128)(2,1)S(1)}, bf16[16,128,128]{2,1,0:T(8,128)(2,1)S(1)}, u32[]{:S(2)}, u32[]{:S(2)}) collective-permute-start(bf16[16,128,128]{2,1,0:T(8,128)(2,1)S(1)} %all_to_all.41.own_ref), channel_id=1, source_target_pairs={{0,1},{1,0},{2,3},{3,2},{4,5},{5,4},{6,7},{7,6},{8,9},{9,8},{10,11... | collective-permute-start | bytes 1572872 | tf_op jit(solution)/shard_map/ppermute | solution.py:75
  87.2 0.1 copy.35
  87.3 0.1 pad_add_fusion.where_ref
  87.4 5.1 %all-gather.2.cloned.1.call-done = bf16[2048,1280]{1,0:T(8,128)(2,1)} async-done(((bf16[128,1280]{1,0:T(8,128)(2,1)}), bf16[2048,1280]{1,0:T(8,128)(2,1)}) %all-gather.2.cloned.1.call-update) | async-done | bytes 5242896 | tf_op jit(solution)/shard_map/all_gather | solution.py:220
  92.5 1.5 dynamic-slice_bitcast_fusion.2
  94.0 1.0 shard_map.109
  95.0 0.2 broadcast_in_dim.8
  95.2 17.8 %all_to_all.42 = bf16[16,256,128]{2,1,0:T(8,128)(2,1)S(1)} all-to-all(bf16[16,256,128]{2,1,0:T(8,128)(2,1)S(1)} %bitcast.110), channel_id=1, replica_groups=mesh['z'=16,'xl'=2,'y'=4,'xh'=2,'core'=2] {'xl','y','xh'}, dimensions={0} | all-to-all | bytes 2097152 | tf_op jit(solution)/shard_map/all_to_all | solution.py:83
  113.0 0.1 add_convert_fusion.1.parts_ref.own_ref
  113.1 10.1 %collective-permute-start.1 = (bf16[8,256,128]{2,1,0:T(8,128)(2,1)S(1)}, bf16[8,256,128]{2,1,0:T(8,128)(2,1)S(1)}, u32[]{:S(2)}, u32[]{:S(2)}) collective-permute-start(bf16[8,256,128]{2,1,0:T(8,128)(2,1)S(1)} %add_convert_fusion.1.parts_ref.own_ref), channel_id=1, source_target_pairs={{0,1},{1,0},{2,3},{3,2},{4,5},{5,4},{6,7},{7,6},{8,9},{9,8},{10,11... | collective-permute-start | bytes 1572872 | tf_op jit(solution)/shard_map/ppermute | solution.py:75
  123.2 0.6 dynamic-slice_bitcast_fusion
  123.8 0.0 copy-start
  123.8 1.3 shard_map.110
  125.1 0.0 collective-permute-done.1.parts_ref
  125.1 1.0 shard_map.112
  126.1 2.2 %collective-permute-start.2 = (bf16[160,1024]{1,0:T(8,128)(2,1)S(1)}, bf16[160,1024]{1,0:T(8,128)(2,1)S(1)}, u32[]{:S(2)}, u32[]{:S(2)}) collective-permute-start(bf16[160,1024]{1,0:T(8,128)(2,1)S(1)} %shard_map.112), channel_id=1, source_target_pairs={{0,16},{16,0},{1,17},{17,1},{2,18},{18,2},{3,19},{19,3},{4,20},{20... | collective-permute-start | bytes 983048 | tf_op jit(solution)/shard_map/ppermute | solution.py:75
  128.3 1.0 shard_map.111
  129.3 8.0 %collective-permute-done.2.far_ref = bf16[160,1024]{1,0:T(8,128)(2,1)S(1)} collective-permute-done((bf16[160,1024]{1,0:T(8,128)(2,1)S(1)}, bf16[160,1024]{1,0:T(8,128)(2,1)S(1)}, u32[]{:S(2)}, u32[]{:S(2)}) %collective-permute-start.2) | collective-permute-done | bytes 327712 | tf_op jit(solution)/shard_map/ppermute | solution.py:75
  137.3 1.2 shard_map.113
  138.4 2.7 %collective-permute-start.3 = (bf16[8,128,256]{2,1,0:T(8,128)(2,1)S(1)}, bf16[8,128,256]{2,1,0:T(8,128)(2,1)S(1)}, u32[]{:S(2)}, u32[]{:S(2)}) collective-permute-start(bf16[8,128,256]{2,1,0:T(8,128)(2,1)S(1)} %get-tuple-element.30), channel_id=1, source_target_pairs={{0,1},{1,0},{2,3},{3,2},{4,5},{5,4},{6,7},{7,6},{8,9},{9,8},{10,11... | collective-permute-start | bytes 1572872 | tf_op jit(solution)/shard_map/ppermute | solution.py:75
  141.2 1.0 shard_map.114
  142.2 0.5 collective-permute-done.3
  142.7 0.1 add_convert_fusion
  142.8 13.5 %all_to_all.43.parts_ref = bf16[8,128,256]{2,1,0:T(8,128)(2,1)S(1)} all-to-all(bf16[8,128,256]{2,1,0:T(8,128)(2,1)S(1)} %add_convert_fusion), channel_id=1, replica_groups=mesh['z'=16,'xl'=2,'y'=4,'xh'=2,'core'=2] {'y','xh'}, dimensions={0} | all-to-all | bytes 1048576 | tf_op jit(solution)/shard_map/all_to_all | solution.py:309
  156.3 1.3 shard_map.115
  (10 shorter events, 0.1 us)
Async XLA Ops:
  6.5 86.0 %all-gather.2.cloned.1.call-start = ((), (), s32[]{:S(2)}) async-start(), calls=%async_computation.5 | async-start | bytes 5570560 | tf_op jit(solution)/shard_map/all_gather | solution.py:220
  9.8 29.6 %all-to-all-start = ((bf16[32,8,128]{2,1,0:T(8,128)(2,1)}), bf16[32,8,128]{2,1,0:T(8,128)(2,1)S(1)}, u32[]{:S(2)}, u32[]{:S(2)}) async-start(bf16[32,8,128]{2,1,0:T(8,128)(2,1)} %fusion.22), calls=%async_computation | async-start | bytes 131072 | tf_op jit(solution)/shard_map/all_to_all | solution.py:229
  33.1 19.9 %copy-start.4 = (f32[4096]{0:T(1024)S(1)}, f32[4096]{0:T(1024)}, u32[]{:S(2)}) copy-start(f32[4096]{0:T(1024)} %param.17) | copy-start | bytes 49156
  33.1 32.7 %copy-start.2 = (bf16[256,128]{1,0:T(8,128)(2,1)S(1)}, bf16[256,128]{1,0:T(8,128)(2,1)}, u32[]{:S(2)}) copy-start(bf16[256,128]{1,0:T(8,128)(2,1)} %param.11) | copy-start | bytes 196612
  40.9 46.3 %copy-start.3 = (bf16[256,128]{1,0:T(8,128)(2,1)S(1)}, bf16[256,128]{1,0:T(8,128)(2,1)}, u32[]{:S(2)}) copy-start(bf16[256,128]{1,0:T(8,128)(2,1)} %param.16) | copy-start | bytes 196612
  46.8 19.0 %all-to-all-start.1 = ((bf16[8,32,128]{2,0,1:T(8,128)(2,1)}), bf16[8,32,128]{2,0,1:T(8,128)(2,1)S(1)}, u32[]{:S(2)}, u32[]{:S(2)}) async-start(bf16[8,32,128]{2,0,1:T(8,128)(2,1)} %copy.33), calls=%async_computation.1 | async-start | bytes 131072 | tf_op jit(solution)/shard_map/all_to_all | solution.py:238
  81.3 12.7 %collective-permute-start = (bf16[16,128,128]{2,1,0:T(8,128)(2,1)S(1)}, bf16[16,128,128]{2,1,0:T(8,128)(2,1)S(1)}, u32[]{:S(2)}, u32[]{:S(2)}) collective-permute-start(bf16[16,128,128]{2,1,0:T(8,128)(2,1)S(1)} %all_to_all.41.own_ref), channel_id=1, source_target_pairs={{0,1},{1,0},{2,3},{3,2},{4,5},{5,4},{6,7},{7,6},{8,9},{9,8},{10,11... | collective-permute-start | bytes 1572872 | tf_op jit(solution)/shard_map/ppermute | solution.py:75
  92.5 30.7 %copy-start.1 = (bf16[2048,1280]{1,0:T(8,128)(2,1)S(1)}, bf16[2048,1280]{1,0:T(8,128)(2,1)}, u32[]{:S(2)}) copy-start(bf16[2048,1280]{1,0:T(8,128)(2,1)} %all-gather.2.cloned.1.call-done) | copy-start | bytes 15728644
  113.1 11.9 %collective-permute-start.1 = (bf16[8,256,128]{2,1,0:T(8,128)(2,1)S(1)}, bf16[8,256,128]{2,1,0:T(8,128)(2,1)S(1)}, u32[]{:S(2)}, u32[]{:S(2)}) collective-permute-start(bf16[8,256,128]{2,1,0:T(8,128)(2,1)S(1)} %add_convert_fusion.1.parts_ref.own_ref), channel_id=1, source_target_pairs={{0,1},{1,0},{2,3},{3,2},{4,5},{5,4},{6,7},{7,6},{8,9},{9,8},{10,11... | collective-permute-start | bytes 1572872 | tf_op jit(solution)/shard_map/ppermute | solution.py:75
  123.8 13.5 %copy-start = (bf16[512,4096]{1,0:T(8,128)(2,1)S(1)}, bf16[512,4096]{1,0:T(8,128)(2,1)}, u32[]{:S(2)}) copy-start(bf16[512,4096]{1,0:T(8,128)(2,1)} %w_ref.3) | copy-start | bytes 12582916
  126.1 11.2 %collective-permute-start.2 = (bf16[160,1024]{1,0:T(8,128)(2,1)S(1)}, bf16[160,1024]{1,0:T(8,128)(2,1)S(1)}, u32[]{:S(2)}, u32[]{:S(2)}) collective-permute-start(bf16[160,1024]{1,0:T(8,128)(2,1)S(1)} %shard_map.112), channel_id=1, source_target_pairs={{0,16},{16,0},{1,17},{17,1},{2,18},{18,2},{3,19},{19,3},{4,20},{20... | collective-permute-start | bytes 983048 | tf_op jit(solution)/shard_map/ppermute | solution.py:75
  138.4 4.3 %collective-permute-start.3 = (bf16[8,128,256]{2,1,0:T(8,128)(2,1)S(1)}, bf16[8,128,256]{2,1,0:T(8,128)(2,1)S(1)}, u32[]{:S(2)}, u32[]{:S(2)}) collective-permute-start(bf16[8,128,256]{2,1,0:T(8,128)(2,1)S(1)} %get-tuple-element.30), channel_id=1, source_target_pairs={{0,1},{1,0},{2,3},{3,2},{4,5},{5,4},{6,7},{7,6},{8,9},{9,8},{10,11... | collective-permute-start | bytes 1572872 | tf_op jit(solution)/shard_map/ppermute | solution.py:75
Sparse Core Ops, SparseCore 0:
  9.4 83.0 all-gather.1

commit v5 on v3

--- a/solution.py
+++ b/solution.py
@@ -104,7 +104,7 @@
     out_ref[1] = total_ref[:, 128:].astype(jnp.bfloat16)
 
 
-def half_ffw(tokens, parts_ref, gain_ref, w_ref):
+def half_ffw(tokens, owner, parts_ref, gain_ref, w_ref):
     total, power = 0.0, 0.0
     for i in range(4):
         wide = jnp.concatenate([parts_ref[2 * i, tokens], parts_ref[2 * i + 1, tokens]], axis=1)
@@ -113,21 +113,23 @@
         scaled = wide * gain_ref[:, i * 256 : i * 256 + 256]
         total += jnp.dot(
             scaled.astype(jnp.bfloat16),
-            w_ref[2 * i : 2 * i + 2].reshape(256, 1024),
+            w_ref[2 * i : 2 * i + 2, owner, :, :1024].reshape(256, 1024),
             preferred_element_type=jnp.float32,
         )
     return total, jnp.broadcast_to(power, (power.shape[0], 128))
 
 
 def first_kernel(where_ref, parts_ref, gain_ref, w_ref, total_ref, power_ref):
-    total_ref[...], power_ref[...] = half_ffw(pl.ds(0, 256), parts_ref, gain_ref, w_ref)
+    total_ref[...], power_ref[...] = half_ffw(
+        pl.ds(0, 256), where_ref[0], parts_ref, gain_ref, w_ref
+    )
 
 
 def far_kernel(
     where_ref, parts_ref, gain_ref, begun_ref, power_ref, own_ref, w_ref, out_ref
 ):
     far = pl.ds(pl.multiple_of((1 - where_ref[1]) * 128, 128), 128)
-    total, power = half_ffw(far, parts_ref, gain_ref, w_ref)
+    total, power = half_ffw(far, 1 - where_ref[0], parts_ref, gain_ref, w_ref)
     out_ref[:128] = (total + begun_ref[far]).astype(jnp.bfloat16)
     row = (power + power_ref[far]).T[:16]
     high = row.astype(jnp.bfloat16)
@@ -141,7 +143,7 @@
     where_ref, parts_ref, gain_ref, begun_ref, power_ref, w_ref, total_ref, own_power_ref
 ):
     near = pl.ds(pl.multiple_of(where_ref[1] * 128, 128), 128)
-    total, power = half_ffw(near, parts_ref, gain_ref, w_ref)
+    total, power = half_ffw(near, 1 - where_ref[0], parts_ref, gain_ref, w_ref)
     total_ref[...] = total + begun_ref[near]
     own_power_ref[...] = power + power_ref[near]
 
@@ -229,6 +231,10 @@
     convolved = inverse_dft(joint_re, joint_im, tables, length).astype(jnp.bfloat16)
     convolved = lax.all_to_all(convolved, ROW, split_axis=1, concat_axis=0, tiled=True)
     gated = (q_stream.astype(jnp.float32) * convolved.astype(jnp.float32)).astype(jnp.bfloat16)
+    gains = lax.dynamic_index_in_dim(norm_gain.reshape(8, 2, 2, 128), side, 2, keepdims=False)
+    gain_own = lax.dynamic_index_in_dim(gains, core, 1, keepdims=False).reshape(1, 1024)
+    gain_other = lax.dynamic_index_in_dim(gains, 1 - core, 1, keepdims=False).reshape(1, 1024)
+    gated, gain_own, gain_other = lax.optimization_barrier((gated, gain_own, gain_other))
     halves = gated.T.reshape(128, 2, 128).transpose(1, 0, 2)[:, None]
     own = gather_plane(jnp.broadcast_to(halves, (2, 8, 128, 128)).reshape(16, 128, 128))
     other = swap(own, "core")
@@ -251,15 +257,11 @@
     weights = after(weights, pairs)
     pairs = pairs.reshape(2, 8, 256, 128)
     own = (pairs[0].astype(jnp.float32) + pairs[1].astype(jnp.float32)).astype(jnp.bfloat16)
-    w_own, w_other = rows_of(weights, core, 0, 1024), rows_of(weights, 1 - core, 0, 1024)
     other = swap(own, "core")
-    gains = lax.dynamic_index_in_dim(norm_gain.reshape(8, 2, 2, 128), side, 2, keepdims=False)
-    gain_own = lax.dynamic_index_in_dim(gains, core, 1, keepdims=False).reshape(1, 1024)
-    gain_other = lax.dynamic_index_in_dim(gains, 1 - core, 1, keepdims=False).reshape(1, 1024)
     begun, power = local_call(
         first_kernel,
         where,
-        (own, gain_own, w_own),
+        (own, gain_own, weights),
         [((256, 1024), jnp.float32), ((256, 128), jnp.float32)],
         2 * 256 * 1024 * 1024,
     )
@@ -267,14 +269,14 @@
     far = local_call(
         far_kernel,
         where,
-        (other, gain_other, begun, power, own, w_other),
+        (other, gain_other, begun, power, own, weights),
         [((160, 1024), jnp.bfloat16)],
         2 * 128 * 1024 * 1024,
     )[0]
     near, power = local_call(
         near_kernel,
         where,
-        (other, gain_other, begun, power, w_other),
+        (other, gain_other, begun, power, weights),
         [((128, 1024), jnp.float32), ((128, 128), jnp.float32)],
         2 * 128 * 1024 * 1024,
     )

time: 169 us -> 165 us (0.976)
  local copies, waits for them, and re-layouts: 8.24 us -> 5.27 us
  blocking collectives: 48.9 us -> 46.9 us
    all_to_all x1 -> x0, blocking collectives: 19.2 us -> none  [on_device(): lax.all_to_all(convolved, ROW, split_axis=1, concat_axis=0, tiled=True)]
    all_to_all x1 -> x2, blocking collectives: 15.4 us -> 33.4 us  [gather_plane(): lax.all_to_all(spread, ('xl', 'y', 'xh'), split_axis=0, concat_axis=0, ti...]
    reshape x2 -> x1, local copies, waits for them, and re-layouts: 4.04 us -> 1.46 us  [rows_of(): return part.reshape(8, 128, width)]
  transfers between devices with their start and end apart: 7 -> 7, of which waited for: 5 -> 6; matrix products, arithmetic and copies ran while one was open for 11% -> 10% of each run, Pallas kernels for 2% -> 2%
where the time goes in v5:
time: 165 us; the launch traced here: 164 us
  blocking collectives  46.9 us (28%)
  starting transfers between devices  44.5 us (27%)
  waiting for transfers between devices  32.4 us (20%)
  between operations  13.8 us (8%)
  matrix products  10 us (6%)
  Pallas kernels  6.52 us (4%)
  local copies, waits for them, and re-layouts  5.27 us (3%)
  other arithmetic  4.64 us (3%)
    all_to_all x2, blocking collectives, gather_plane(): lax.all_to_all(spread, ('xl', 'y', 'xh'), split_axis=0, concat_axis=0, ti...  33.4 us
    ppermute x4, starting transfers between devices, swap(): return lax.ppermute(array, axis, [(0, 1), (1, 0)])  21.3 us
    all_to_all x1, starting transfers between devices, on_device(): lax.all_to_all(product, ROW, split_axis=0, concat_axis=1, tiled=True)  17 us
    all_to_all x1, blocking collectives, on_device(): lax.all_to_all(down, ('y', 'xh'), split_axis=0, concat_axis=0, tiled=True)  13.5 us
    all_to_all x1, waiting for transfers between devices, on_device(): lax.all_to_all(convolved, ROW, split_axis=1, concat_axis=0, tiled=True)  12.6 us
    ppermute x4, waiting for transfers between devices, swap(): return lax.ppermute(array, axis, [(0, 1), (1, 0)])  8.3 us
    dot_general x12, matrix products, apply_last(): jnp.einsum('ckn,nm->ckm', blocks, matrix, precision=lax.Precision.HIGHEST)  7.42 us
    pallas_call x6, Pallas kernels, local_call(): pl.pallas_call(kernel, in_specs=[pl.BlockSpec(memory_space=pltpu.SMEM)] +...  6.52 us
  transfers between devices with their start and end apart: 7, of which 6 were waited for; matrix products, arithmetic and copies ran while one was open for 10% of the time, Pallas kernels for 2%

profile of v5, /device:TPU:1, one launch (start us, length us, event | category | flops | bytes accessed | tf_op | source)
XLA Modules:
  0.0 164.0 jit_solution(11489945865254293723)
XLA Ops:
  6.5 1.8 %pad_maximum_fusion = bf16[128,1280]{1,0:T(8,128)(2,1)} fusion(bf16[128,256]{1,0:T(8,128)(2,1)} %param.18, bf16[128,512]{1,0:T(8,128)(2,1)} %param.20, bf16[128,512]{1,0:T(8,128)(2,1)} %param.19), kind=kLoop, calls=%fused_computation.19 | loop fusion | flops 983040 | bytes 655360 | tf_op jit(solution)/shard_map/concatenate | solution.py:215
  8.3 0.0 all-gather.2.cloned.1.call-update
  8.3 1.5 fusion.22
  9.9 17.0 %all-to-all-start = ((bf16[32,8,128]{2,1,0:T(8,128)(2,1)}), bf16[32,8,128]{2,1,0:T(8,128)(2,1)S(1)}, u32[]{:S(2)}, u32[]{:S(2)}) async-start(bf16[32,8,128]{2,1,0:T(8,128)(2,1)} %fusion.22), calls=%async_computation | async-start | bytes 131072 | tf_op jit(solution)/shard_map/all_to_all | solution.py:223
  26.8 0.7 slice.14
  27.5 1.0 slice.15
  28.5 0.1 copy.31
  28.6 0.7 bitcast_add_fusion
  29.3 0.1 copy.26
  29.3 0.1 sine_negate_fusion.7
  29.5 0.1 maximum_bitcast_fusion
  29.6 0.5 convolution_bitcast_fusion
  30.1 0.5 convolution_bitcast_fusion.1
  30.6 0.6 fusion.26
  31.2 0.6 convolution_add_fusion.1
  31.9 0.6 fusion.38
  32.5 0.6 convolution_subtract_fusion.1
  33.1 0.0 copy-start.4
  33.1 0.0 copy-start.2
  33.1 6.3 %all-to-all-done = bf16[32,8,128]{2,1,0:T(8,128)(2,1)S(1)} async-done(((bf16[32,8,128]{2,1,0:T(8,128)(2,1)}), bf16[32,8,128]{2,1,0:T(8,128)(2,1)S(1)}, u32[]{:S(2)}, u32[]{:S(2)}) %all-to-all-start) | async-done | bytes 65568 | tf_op jit(solution)/shard_map/all_to_all | solution.py:223
  39.5 0.4 convolution_bitcast_fusion.2
  39.9 0.4 convolution_bitcast_fusion.3
  40.3 0.6 fusion.28
  40.9 0.0 copy-start.3
  40.9 0.6 fusion.40
  41.5 0.6 convolution_subtract_fusion.2
  42.1 0.7 multiply_subtract_fusion
  42.8 0.6 fusion.34
  43.4 0.6 fusion.32
  44.0 0.6 convolution_add_fusion
  44.7 0.6 convolution_subtract_fusion
  45.3 0.4 fusion.6
  45.7 0.4 fusion.2
  46.1 0.7 copy.27
  46.8 6.2 %all-to-all-start.1 = ((bf16[8,32,128]{2,0,1:T(8,128)(2,1)}), bf16[8,32,128]{2,0,1:T(8,128)(2,1)S(1)}, u32[]{:S(2)}, u32[]{:S(2)}) async-start(bf16[8,32,128]{2,0,1:T(8,128)(2,1)} %copy.27), calls=%async_computation.1 | async-start | bytes 131072 | tf_op jit(solution)/shard_map/all_to_all | solution.py:232
  53.0 12.6 %all-to-all-done.1 = bf16[8,32,128]{2,0,1:T(8,128)(2,1)S(1)} async-done(((bf16[8,32,128]{2,0,1:T(8,128)(2,1)}), bf16[8,32,128]{2,0,1:T(8,128)(2,1)S(1)}, u32[]{:S(2)}, u32[]{:S(2)}) %all-to-all-start.1) | async-done | bytes 65568 | tf_op jit(solution)/shard_map/all_to_all | solution.py:232
  65.7 0.1 copy.28
  65.8 0.1 broadcast_in_dim.7
  65.9 15.4 %all_to_all.41.own_ref = bf16[16,128,128]{2,1,0:T(8,128)(2,1)S(1)} all-to-all(bf16[16,128,128]{2,1,0:T(8,128)(2,1)S(1)} %bitcast.107), channel_id=1, replica_groups=mesh['z'=16,'xl'=2,'y'=4,'xh'=2,'core'=2] {'xl','y','xh'}, dimensions={0} | all-to-all | bytes 1048576 | tf_op jit(solution)/shard_map/all_to_all | solution.py:83
  81.3 5.9 %collective-permute-start = (bf16[16,128,128]{2,1,0:T(8,128)(2,1)S(1)}, bf16[16,128,128]{2,1,0:T(8,128)(2,1)S(1)}, u32[]{:S(2)}, u32[]{:S(2)}) collective-permute-start(bf16[16,128,128]{2,1,0:T(8,128)(2,1)S(1)} %all_to_all.41.own_ref), channel_id=1, source_target_pairs={{0,1},{1,0},{2,3},{3,2},{4,5},{5,4},{6,7},{7,6},{8,9},{9,8},{10,11... | collective-permute-start | bytes 1572872 | tf_op jit(solution)/shard_map/ppermute | solution.py:75
  87.2 0.1 copy.29
  87.3 0.1 pad_add_fusion.where_ref
  87.4 5.1 %all-gather.2.cloned.1.call-done = bf16[2048,1280]{1,0:T(8,128)(2,1)} async-done(((bf16[128,1280]{1,0:T(8,128)(2,1)}), bf16[2048,1280]{1,0:T(8,128)(2,1)}) %all-gather.2.cloned.1.call-update) | async-done | bytes 5242896 | tf_op jit(solution)/shard_map/all_gather | solution.py:214
  92.5 1.5 dynamic-slice_bitcast_fusion
  94.0 1.0 shard_map.109
  95.0 0.2 broadcast_in_dim.8
  95.2 18.0 %all_to_all.42 = bf16[16,256,128]{2,1,0:T(8,128)(2,1)S(1)} all-to-all(bf16[16,256,128]{2,1,0:T(8,128)(2,1)S(1)} %bitcast.106), channel_id=1, replica_groups=mesh['z'=16,'xl'=2,'y'=4,'xh'=2,'core'=2] {'xl','y','xh'}, dimensions={0} | all-to-all | bytes 2097152 | tf_op jit(solution)/shard_map/all_to_all | solution.py:83
  113.2 0.1 add_convert_fusion.1.parts_ref.own_ref
  113.4 9.9 %collective-permute-start.1 = (bf16[8,256,128]{2,1,0:T(8,128)(2,1)S(1)}, bf16[8,256,128]{2,1,0:T(8,128)(2,1)S(1)}, u32[]{:S(2)}, u32[]{:S(2)}) collective-permute-start(bf16[8,256,128]{2,1,0:T(8,128)(2,1)S(1)} %add_convert_fusion.1.parts_ref.own_ref), channel_id=1, source_target_pairs={{0,1},{1,0},{2,3},{3,2},{4,5},{5,4},{6,7},{7,6},{8,9},{9,8},{10,11... | collective-permute-start | bytes 1572872 | tf_op jit(solution)/shard_map/ppermute | solution.py:75
  123.3 1.3 shard_map.110
  124.6 0.2 collective-permute-done.1.parts_ref
  124.8 1.0 shard_map.112
  125.8 0.0 copy-start.1
  125.8 2.5 %collective-permute-start.2 = (bf16[160,1024]{1,0:T(8,128)(2,1)S(1)}, bf16[160,1024]{1,0:T(8,128)(2,1)S(1)}, u32[]{:S(2)}, u32[]{:S(2)}) collective-permute-start(bf16[160,1024]{1,0:T(8,128)(2,1)S(1)} %shard_map.112), channel_id=1, source_target_pairs={{0,16},{16,0},{1,17},{17,1},{2,18},{18,2},{3,19},{19,3},{4,20},{20... | collective-permute-start | bytes 983048 | tf_op jit(solution)/shard_map/ppermute | solution.py:75
  128.3 1.0 shard_map.111
  129.3 7.6 %collective-permute-done.2.far_ref = bf16[160,1024]{1,0:T(8,128)(2,1)S(1)} collective-permute-done((bf16[160,1024]{1,0:T(8,128)(2,1)S(1)}, bf16[160,1024]{1,0:T(8,128)(2,1)S(1)}, u32[]{:S(2)}, u32[]{:S(2)}) %collective-permute-start.2) | collective-permute-done | bytes 327712 | tf_op jit(solution)/shard_map/ppermute | solution.py:75
  136.9 1.2 shard_map.113
  138.1 3.1 %collective-permute-start.3 = (bf16[8,128,256]{2,1,0:T(8,128)(2,1)S(1)}, bf16[8,128,256]{2,1,0:T(8,128)(2,1)S(1)}, u32[]{:S(2)}, u32[]{:S(2)}) collective-permute-start(bf16[8,128,256]{2,1,0:T(8,128)(2,1)S(1)} %get-tuple-element.31), channel_id=1, source_target_pairs={{0,1},{1,0},{2,3},{3,2},{4,5},{5,4},{6,7},{7,6},{8,9},{9,8},{10,11... | collective-permute-start | bytes 1572872 | tf_op jit(solution)/shard_map/ppermute | solution.py:75
  141.2 1.0 shard_map.114
  142.2 0.5 collective-permute-done.3
  142.7 0.1 add_convert_fusion
  142.8 13.5 %all_to_all.43 = bf16[8,128,256]{2,1,0:T(8,128)(2,1)S(1)} all-to-all(bf16[8,128,256]{2,1,0:T(8,128)(2,1)S(1)} %add_convert_fusion), channel_id=1, replica_groups=mesh['z'=16,'xl'=2,'y'=4,'xh'=2,'core'=2] {'y','xh'}, dimensions={0} | all-to-all | bytes 1048576 | tf_op jit(solution)/shard_map/all_to_all | solution.py:302
  156.3 0.1 convert_reduce_fusion
  156.4 0.7 copy.30
  (11 shorter events, 0.1 us)
Async XLA Ops:
  6.5 86.0 %all-gather.2.cloned.1.call-start = ((), (), s32[]{:S(2)}) async-start(), calls=%async_computation.5 | async-start | bytes 5570560 | tf_op jit(solution)/shard_map/all_gather | solution.py:214
  9.9 29.6 %all-to-all-start = ((bf16[32,8,128]{2,1,0:T(8,128)(2,1)}), bf16[32,8,128]{2,1,0:T(8,128)(2,1)S(1)}, u32[]{:S(2)}, u32[]{:S(2)}) async-start(bf16[32,8,128]{2,1,0:T(8,128)(2,1)} %fusion.22), calls=%async_computation | async-start | bytes 131072 | tf_op jit(solution)/shard_map/all_to_all | solution.py:223
  33.1 19.9 %copy-start.4 = (f32[4096]{0:T(1024)S(1)}, f32[4096]{0:T(1024)}, u32[]{:S(2)}) copy-start(f32[4096]{0:T(1024)} %param.17) | copy-start | bytes 49156
  33.1 32.6 %copy-start.2 = (bf16[256,128]{1,0:T(8,128)(2,1)S(1)}, bf16[256,128]{1,0:T(8,128)(2,1)}, u32[]{:S(2)}) copy-start(bf16[256,128]{1,0:T(8,128)(2,1)} %param.11) | copy-start | bytes 196612
  40.9 46.3 %copy-start.3 = (bf16[256,128]{1,0:T(8,128)(2,1)S(1)}, bf16[256,128]{1,0:T(8,128)(2,1)}, u32[]{:S(2)}) copy-start(bf16[256,128]{1,0:T(8,128)(2,1)} %param.16) | copy-start | bytes 196612
  46.8 18.9 %all-to-all-start.1 = ((bf16[8,32,128]{2,0,1:T(8,128)(2,1)}), bf16[8,32,128]{2,0,1:T(8,128)(2,1)S(1)}, u32[]{:S(2)}, u32[]{:S(2)}) async-start(bf16[8,32,128]{2,0,1:T(8,128)(2,1)} %copy.27), calls=%async_computation.1 | async-start | bytes 131072 | tf_op jit(solution)/shard_map/all_to_all | solution.py:232
  81.3 12.7 %collective-permute-start = (bf16[16,128,128]{2,1,0:T(8,128)(2,1)S(1)}, bf16[16,128,128]{2,1,0:T(8,128)(2,1)S(1)}, u32[]{:S(2)}, u32[]{:S(2)}) collective-permute-start(bf16[16,128,128]{2,1,0:T(8,128)(2,1)S(1)} %all_to_all.41.own_ref), channel_id=1, source_target_pairs={{0,1},{1,0},{2,3},{3,2},{4,5},{5,4},{6,7},{7,6},{8,9},{9,8},{10,11... | collective-permute-start | bytes 1572872 | tf_op jit(solution)/shard_map/ppermute | solution.py:75
  92.5 30.8 %copy-start = (bf16[2048,1280]{1,0:T(8,128)(2,1)S(1)}, bf16[2048,1280]{1,0:T(8,128)(2,1)}, u32[]{:S(2)}) copy-start(bf16[2048,1280]{1,0:T(8,128)(2,1)} %all-gather.2.cloned.1.call-done) | copy-start | bytes 15728644
  113.4 11.4 %collective-permute-start.1 = (bf16[8,256,128]{2,1,0:T(8,128)(2,1)S(1)}, bf16[8,256,128]{2,1,0:T(8,128)(2,1)S(1)}, u32[]{:S(2)}, u32[]{:S(2)}) collective-permute-start(bf16[8,256,128]{2,1,0:T(8,128)(2,1)S(1)} %add_convert_fusion.1.parts_ref.own_ref), channel_id=1, source_target_pairs={{0,1},{1,0},{2,3},{3,2},{4,5},{5,4},{6,7},{7,6},{8,9},{9,8},{10,11... | collective-permute-start | bytes 1572872 | tf_op jit(solution)/shard_map/ppermute | solution.py:75
  125.8 11.1 %copy-start.1 = (bf16[512,4096]{1,0:T(8,128)(2,1)S(1)}, bf16[512,4096]{1,0:T(8,128)(2,1)}, u32[]{:S(2)}) copy-start(bf16[512,4096]{1,0:T(8,128)(2,1)} %w_ref.3) | copy-start | bytes 12582916
  125.8 11.1 %collective-permute-start.2 = (bf16[160,1024]{1,0:T(8,128)(2,1)S(1)}, bf16[160,1024]{1,0:T(8,128)(2,1)S(1)}, u32[]{:S(2)}, u32[]{:S(2)}) collective-permute-start(bf16[160,1024]{1,0:T(8,128)(2,1)S(1)} %shard_map.112), channel_id=1, source_target_pairs={{0,16},{16,0},{1,17},{17,1},{2,18},{18,2},{3,19},{19,3},{4,20},{20... | collective-permute-start | bytes 983048 | tf_op jit(solution)/shard_map/ppermute | solution.py:75
  138.1 4.6 %collective-permute-start.3 = (bf16[8,128,256]{2,1,0:T(8,128)(2,1)S(1)}, bf16[8,128,256]{2,1,0:T(8,128)(2,1)S(1)}, u32[]{:S(2)}, u32[]{:S(2)}) collective-permute-start(bf16[8,128,256]{2,1,0:T(8,128)(2,1)S(1)} %get-tuple-element.31), channel_id=1, source_target_pairs={{0,1},{1,0},{2,3},{3,2},{4,5},{5,4},{6,7},{7,6},{8,9},{9,8},{10,11... | collective-permute-start | bytes 1572872 | tf_op jit(solution)/shard_map/ppermute | solution.py:75
Sparse Core Ops, SparseCore 0:
  9.4 83.0 all-gather.1

commit v6 on v5

--- a/solution.py
+++ b/solution.py
@@ -149,7 +149,8 @@
 
 
 def columns_of(w_ref, index, core):
-    return w_ref[:, pl.ds(pl.multiple_of((2 * index + core) * 256, 256), 256)]
+    column = 2 * (index % 4) + index // 4
+    return w_ref[:, pl.ds(pl.multiple_of((2 * column + core) * 256, 256), 256)]
 
 
 def down_far_kernel(
@@ -252,11 +253,12 @@
         2 * 256 * 256 * 2048,
         [pltpu.VMEM((256, 256), jnp.float32)],
     )[0]
-    spread = jnp.broadcast_to(mixed[:, None], (2, 8, 256, 128)).reshape(16, 256, 128)
-    pairs = gather_plane(spread)
+    spread = jnp.broadcast_to(mixed[None, :, None], (4, 2, 2, 256, 128)).reshape(16, 256, 128)
+    pairs = lax.all_to_all(spread, ("y", "xl", "xh"), split_axis=0, concat_axis=0, tiled=True)
     weights = after(weights, pairs)
-    pairs = pairs.reshape(2, 8, 256, 128)
-    own = (pairs[0].astype(jnp.float32) + pairs[1].astype(jnp.float32)).astype(jnp.bfloat16)
+    pairs = pairs.reshape(4, 2, 2, 256, 128)
+    own = (pairs[:, 0].astype(jnp.float32) + pairs[:, 1].astype(jnp.float32)).astype(jnp.bfloat16)
+    own = own.reshape(8, 256, 128)
     other = swap(own, "core")
     begun, power = local_call(
         first_kernel,
@@ -301,7 +303,7 @@
     down = (near + far.astype(jnp.float32)).astype(jnp.bfloat16)
     parts = lax.all_to_all(
         down,
-        ("y", "xh"),
+        ("xh", "y"),
         split_axis=0,
         concat_axis=0,
         tiled=True,

time: 165 us -> 164 us (level)
    all_to_all x2 -> x1, blocking collectives: 33.4 us -> 15.4 us  [gather_plane(): lax.all_to_all(spread, ('xl', 'y', 'xh'), split_axis=0, concat_axis=0, ti...]
    all_to_all x1 -> x2, blocking collectives: 13.5 us -> 30.7 us  [the longest x1 17.9 us: on_device(): lax.all_to_all(spread, ('y', 'xl', 'xh'), split_axis=0, concat_axis=0, ti...]
where the time goes in v6:
time: 164 us; the launch traced here: 163 us
  blocking collectives  46.1 us (28%)
  starting transfers between devices  44.3 us (27%)
  waiting for transfers between devices  32.7 us (20%)
  between operations  13.8 us (8%)
  matrix products  10 us (6%)
  Pallas kernels  6.53 us (4%)
  local copies, waits for them, and re-layouts  5.27 us (3%)
  other arithmetic  4.64 us (3%)
    ppermute x4, starting transfers between devices, swap(): return lax.ppermute(array, axis, [(0, 1), (1, 0)])  21.1 us
    all_to_all x1, blocking collectives, on_device(): lax.all_to_all(spread, ('y', 'xl', 'xh'), split_axis=0, concat_axis=0, ti...  17.9 us
    all_to_all x1, starting transfers between devices, on_device(): lax.all_to_all(product, ROW, split_axis=0, concat_axis=1, tiled=True)  17 us
    all_to_all x1, blocking collectives, gather_plane(): lax.all_to_all(spread, ('xl', 'y', 'xh'), split_axis=0, concat_axis=0, ti...  15.4 us
    all_to_all x1, blocking collectives, on_device(): lax.all_to_all(down, ('xh', 'y'), split_axis=0, concat_axis=0, tiled=True)  12.8 us
    all_to_all x1, waiting for transfers between devices, on_device(): lax.all_to_all(convolved, ROW, split_axis=1, concat_axis=0, tiled=True)  12.6 us
    ppermute x4, waiting for transfers between devices, swap(): return lax.ppermute(array, axis, [(0, 1), (1, 0)])  8.53 us
    dot_general x12, matrix products, apply_last(): jnp.einsum('ckn,nm->ckm', blocks, matrix, precision=lax.Precision.HIGHEST)  7.42 us
  transfers between devices with their start and end apart: 7, of which 6 were waited for; matrix products, arithmetic and copies ran while one was open for 10% of the time, Pallas kernels for 2%

profile of v6, /device:TPU:1, one launch (start us, length us, event | category | flops | bytes accessed | tf_op | source)
XLA Modules:
  0.0 163.2 jit_solution(17817985466166659530)
XLA Ops:
  6.5 1.8 %pad_maximum_fusion = bf16[128,1280]{1,0:T(8,128)(2,1)} fusion(bf16[128,256]{1,0:T(8,128)(2,1)} %param.18, bf16[128,512]{1,0:T(8,128)(2,1)} %param.20, bf16[128,512]{1,0:T(8,128)(2,1)} %param.19), kind=kLoop, calls=%fused_computation.19 | loop fusion | flops 983040 | bytes 655360 | tf_op jit(solution)/shard_map/concatenate | solution.py:216
  8.3 0.0 all-gather.2.cloned.1.call-update
  8.3 1.5 fusion.22
  9.9 17.0 %all-to-all-start = ((bf16[32,8,128]{2,1,0:T(8,128)(2,1)}), bf16[32,8,128]{2,1,0:T(8,128)(2,1)S(1)}, u32[]{:S(2)}, u32[]{:S(2)}) async-start(bf16[32,8,128]{2,1,0:T(8,128)(2,1)} %fusion.22), calls=%async_computation | async-start | bytes 131072 | tf_op jit(solution)/shard_map/all_to_all | solution.py:224
  26.8 0.7 slice.12
  27.5 1.0 slice.13
  28.5 0.1 copy.31
  28.6 0.7 bitcast_add_fusion
  29.3 0.1 copy.26
  29.3 0.1 sine_negate_fusion.7
  29.5 0.1 maximum_bitcast_fusion
  29.6 0.5 convolution_bitcast_fusion
  30.1 0.5 convolution_bitcast_fusion.1
  30.6 0.6 fusion.26
  31.2 0.6 convolution_add_fusion.1
  31.9 0.6 fusion.38
  32.5 0.6 convolution_subtract_fusion.1
  33.1 0.0 copy-start.4
  33.1 0.0 copy-start.2
  33.1 6.3 %all-to-all-done = bf16[32,8,128]{2,1,0:T(8,128)(2,1)S(1)} async-done(((bf16[32,8,128]{2,1,0:T(8,128)(2,1)}), bf16[32,8,128]{2,1,0:T(8,128)(2,1)S(1)}, u32[]{:S(2)}, u32[]{:S(2)}) %all-to-all-start) | async-done | bytes 65568 | tf_op jit(solution)/shard_map/all_to_all | solution.py:224
  39.5 0.4 convolution_bitcast_fusion.2
  39.9 0.4 convolution_bitcast_fusion.3
  40.3 0.6 fusion.28
  40.9 0.0 copy-start.3
  40.9 0.6 fusion.40
  41.5 0.6 convolution_subtract_fusion.2
  42.1 0.7 multiply_subtract_fusion
  42.8 0.6 fusion.34
  43.4 0.6 fusion.32
  44.0 0.6 convolution_add_fusion
  44.7 0.6 convolution_subtract_fusion
  45.3 0.4 fusion.6
  45.7 0.4 fusion.2
  46.1 0.7 copy.27
  46.8 6.2 %all-to-all-start.1 = ((bf16[8,32,128]{2,0,1:T(8,128)(2,1)}), bf16[8,32,128]{2,0,1:T(8,128)(2,1)S(1)}, u32[]{:S(2)}, u32[]{:S(2)}) async-start(bf16[8,32,128]{2,0,1:T(8,128)(2,1)} %copy.27), calls=%async_computation.1 | async-start | bytes 131072 | tf_op jit(solution)/shard_map/all_to_all | solution.py:233
  53.0 12.6 %all-to-all-done.1 = bf16[8,32,128]{2,0,1:T(8,128)(2,1)S(1)} async-done(((bf16[8,32,128]{2,0,1:T(8,128)(2,1)}), bf16[8,32,128]{2,0,1:T(8,128)(2,1)S(1)}, u32[]{:S(2)}, u32[]{:S(2)}) %all-to-all-start.1) | async-done | bytes 65568 | tf_op jit(solution)/shard_map/all_to_all | solution.py:233
  65.7 0.1 copy.28
  65.8 0.1 broadcast_in_dim.7
  65.9 15.4 %all_to_all.41.own_ref = bf16[16,128,128]{2,1,0:T(8,128)(2,1)S(1)} all-to-all(bf16[16,128,128]{2,1,0:T(8,128)(2,1)S(1)} %bitcast.114), channel_id=1, replica_groups=mesh['z'=16,'xl'=2,'y'=4,'xh'=2,'core'=2] {'xl','y','xh'}, dimensions={0} | all-to-all | bytes 1048576 | tf_op jit(solution)/shard_map/all_to_all | solution.py:83
  81.3 5.9 %collective-permute-start = (bf16[16,128,128]{2,1,0:T(8,128)(2,1)S(1)}, bf16[16,128,128]{2,1,0:T(8,128)(2,1)S(1)}, u32[]{:S(2)}, u32[]{:S(2)}) collective-permute-start(bf16[16,128,128]{2,1,0:T(8,128)(2,1)S(1)} %all_to_all.41.own_ref), channel_id=1, source_target_pairs={{0,1},{1,0},{2,3},{3,2},{4,5},{5,4},{6,7},{7,6},{8,9},{9,8},{10,11... | collective-permute-start | bytes 1572872 | tf_op jit(solution)/shard_map/ppermute | solution.py:75
  87.2 0.1 copy.29
  87.3 0.1 pad_add_fusion.where_ref
  87.4 5.1 %all-gather.2.cloned.1.call-done = bf16[2048,1280]{1,0:T(8,128)(2,1)} async-done(((bf16[128,1280]{1,0:T(8,128)(2,1)}), bf16[2048,1280]{1,0:T(8,128)(2,1)}) %all-gather.2.cloned.1.call-update) | async-done | bytes 5242896 | tf_op jit(solution)/shard_map/all_gather | solution.py:215
  92.5 1.5 dynamic-slice_bitcast_fusion
  94.0 1.0 shard_map.109
  95.0 0.2 broadcast_in_dim.8
  95.2 17.9 %all_to_all.42 = bf16[16,256,128]{2,1,0:T(8,128)(2,1)S(1)} all-to-all(bf16[16,256,128]{2,1,0:T(8,128)(2,1)S(1)} %bitcast.112), channel_id=1, replica_groups=mesh['z'=16,'xl'=2,'y'=4,'xh'=2,'core'=2] {'y','xl','xh'}, dimensions={0} | all-to-all | bytes 2097152 | tf_op jit(solution)/shard_map/all_to_all | solution.py:257
  113.1 0.1 add_convert_fusion.1
  113.3 9.9 %collective-permute-start.1 = (bf16[8,256,128]{2,1,0:T(8,128)(2,1)S(1)}, bf16[8,256,128]{2,1,0:T(8,128)(2,1)S(1)}, u32[]{:S(2)}, u32[]{:S(2)}) collective-permute-start(bf16[8,256,128]{2,1,0:T(8,128)(2,1)S(1)} %bitcast.107), channel_id=1, source_target_pairs={{0,1},{1,0},{2,3},{3,2},{4,5},{5,4},{6,7},{7,6},{8,9},{9,8},{10,11... | collective-permute-start | bytes 1572872 | tf_op jit(solution)/shard_map/ppermute | solution.py:75
  123.2 1.3 shard_map.110
  124.5 0.2 collective-permute-done.1.parts_ref
  124.7 1.0 shard_map.112
  125.7 0.0 copy-start.1
  125.7 2.2 %collective-permute-start.2 = (bf16[160,1024]{1,0:T(8,128)(2,1)S(1)}, bf16[160,1024]{1,0:T(8,128)(2,1)S(1)}, u32[]{:S(2)}, u32[]{:S(2)}) collective-permute-start(bf16[160,1024]{1,0:T(8,128)(2,1)S(1)} %shard_map.112), channel_id=1, source_target_pairs={{0,16},{16,0},{1,17},{17,1},{2,18},{18,2},{3,19},{19,3},{4,20},{20... | collective-permute-start | bytes 983048 | tf_op jit(solution)/shard_map/ppermute | solution.py:75
  128.0 1.0 shard_map.111
  129.0 7.8 %collective-permute-done.2.far_ref = bf16[160,1024]{1,0:T(8,128)(2,1)S(1)} collective-permute-done((bf16[160,1024]{1,0:T(8,128)(2,1)S(1)}, bf16[160,1024]{1,0:T(8,128)(2,1)S(1)}, u32[]{:S(2)}, u32[]{:S(2)}) %collective-permute-start.2) | collective-permute-done | bytes 327712 | tf_op jit(solution)/shard_map/ppermute | solution.py:75
  136.8 1.2 shard_map.113
  138.0 3.1 %collective-permute-start.3 = (bf16[8,128,256]{2,1,0:T(8,128)(2,1)S(1)}, bf16[8,128,256]{2,1,0:T(8,128)(2,1)S(1)}, u32[]{:S(2)}, u32[]{:S(2)}) collective-permute-start(bf16[8,128,256]{2,1,0:T(8,128)(2,1)S(1)} %get-tuple-element.31), channel_id=1, source_target_pairs={{0,1},{1,0},{2,3},{3,2},{4,5},{5,4},{6,7},{7,6},{8,9},{9,8},{10,11... | collective-permute-start | bytes 1572872 | tf_op jit(solution)/shard_map/ppermute | solution.py:75
  141.1 1.1 shard_map.114
  142.2 0.5 collective-permute-done.3
  142.6 0.1 add_convert_fusion
  142.8 12.8 %all_to_all.43 = bf16[8,128,256]{2,1,0:T(8,128)(2,1)S(1)} all-to-all(bf16[8,128,256]{2,1,0:T(8,128)(2,1)S(1)} %add_convert_fusion), channel_id=1, replica_groups=mesh['z'=16,'xl'=2,'y'=4,'xh'=2,'core'=2] {'xh','y'}, dimensions={0} | all-to-all | bytes 1048576 | tf_op jit(solution)/shard_map/all_to_all | solution.py:304
  155.6 0.1 convert_reduce_fusion
  155.7 0.7 copy.30
  (11 shorter events, 0.1 us)
Async XLA Ops:
  6.5 86.0 %all-gather.2.cloned.1.call-start = ((), (), s32[]{:S(2)}) async-start(), calls=%async_computation.5 | async-start | bytes 5570560 | tf_op jit(solution)/shard_map/all_gather | solution.py:215
  9.9 29.6 %all-to-all-start = ((bf16[32,8,128]{2,1,0:T(8,128)(2,1)}), bf16[32,8,128]{2,1,0:T(8,128)(2,1)S(1)}, u32[]{:S(2)}, u32[]{:S(2)}) async-start(bf16[32,8,128]{2,1,0:T(8,128)(2,1)} %fusion.22), calls=%async_computation | async-start | bytes 131072 | tf_op jit(solution)/shard_map/all_to_all | solution.py:224
  33.1 19.9 %copy-start.4 = (f32[4096]{0:T(1024)S(1)}, f32[4096]{0:T(1024)}, u32[]{:S(2)}) copy-start(f32[4096]{0:T(1024)} %param.17) | copy-start | bytes 49156
  33.1 32.6 %copy-start.2 = (bf16[256,128]{1,0:T(8,128)(2,1)S(1)}, bf16[256,128]{1,0:T(8,128)(2,1)}, u32[]{:S(2)}) copy-start(bf16[256,128]{1,0:T(8,128)(2,1)} %param.11) | copy-start | bytes 196612
  40.9 46.3 %copy-start.3 = (bf16[256,128]{1,0:T(8,128)(2,1)S(1)}, bf16[256,128]{1,0:T(8,128)(2,1)}, u32[]{:S(2)}) copy-start(bf16[256,128]{1,0:T(8,128)(2,1)} %param.16) | copy-start | bytes 196612
  46.8 18.9 %all-to-all-start.1 = ((bf16[8,32,128]{2,0,1:T(8,128)(2,1)}), bf16[8,32,128]{2,0,1:T(8,128)(2,1)S(1)}, u32[]{:S(2)}, u32[]{:S(2)}) async-start(bf16[8,32,128]{2,0,1:T(8,128)(2,1)} %copy.27), calls=%async_computation.1 | async-start | bytes 131072 | tf_op jit(solution)/shard_map/all_to_all | solution.py:233
  81.3 12.7 %collective-permute-start = (bf16[16,128,128]{2,1,0:T(8,128)(2,1)S(1)}, bf16[16,128,128]{2,1,0:T(8,128)(2,1)S(1)}, u32[]{:S(2)}, u32[]{:S(2)}) collective-permute-start(bf16[16,128,128]{2,1,0:T(8,128)(2,1)S(1)} %all_to_all.41.own_ref), channel_id=1, source_target_pairs={{0,1},{1,0},{2,3},{3,2},{4,5},{5,4},{6,7},{7,6},{8,9},{9,8},{10,11... | collective-permute-start | bytes 1572872 | tf_op jit(solution)/shard_map/ppermute | solution.py:75
  92.5 30.7 %copy-start = (bf16[2048,1280]{1,0:T(8,128)(2,1)S(1)}, bf16[2048,1280]{1,0:T(8,128)(2,1)}, u32[]{:S(2)}) copy-start(bf16[2048,1280]{1,0:T(8,128)(2,1)} %all-gather.2.cloned.1.call-done) | copy-start | bytes 15728644
  113.3 11.5 %collective-permute-start.1 = (bf16[8,256,128]{2,1,0:T(8,128)(2,1)S(1)}, bf16[8,256,128]{2,1,0:T(8,128)(2,1)S(1)}, u32[]{:S(2)}, u32[]{:S(2)}) collective-permute-start(bf16[8,256,128]{2,1,0:T(8,128)(2,1)S(1)} %bitcast.107), channel_id=1, source_target_pairs={{0,1},{1,0},{2,3},{3,2},{4,5},{5,4},{6,7},{7,6},{8,9},{9,8},{10,11... | collective-permute-start | bytes 1572872 | tf_op jit(solution)/shard_map/ppermute | solution.py:75
  125.7 11.1 %copy-start.1 = (bf16[512,4096]{1,0:T(8,128)(2,1)S(1)}, bf16[512,4096]{1,0:T(8,128)(2,1)}, u32[]{:S(2)}) copy-start(bf16[512,4096]{1,0:T(8,128)(2,1)} %w_ref.3) | copy-start | bytes 12582916
  125.7 11.1 %collective-permute-start.2 = (bf16[160,1024]{1,0:T(8,128)(2,1)S(1)}, bf16[160,1024]{1,0:T(8,128)(2,1)S(1)}, u32[]{:S(2)}, u32[]{:S(2)}) collective-permute-start(bf16[160,1024]{1,0:T(8,128)(2,1)S(1)} %shard_map.112), channel_id=1, source_target_pairs={{0,16},{16,0},{1,17},{17,1},{2,18},{18,2},{3,19},{19,3},{4,20},{20... | collective-permute-start | bytes 983048 | tf_op jit(solution)/shard_map/ppermute | solution.py:75
  138.0 4.6 %collective-permute-start.3 = (bf16[8,128,256]{2,1,0:T(8,128)(2,1)S(1)}, bf16[8,128,256]{2,1,0:T(8,128)(2,1)S(1)}, u32[]{:S(2)}, u32[]{:S(2)}) collective-permute-start(bf16[8,128,256]{2,1,0:T(8,128)(2,1)S(1)} %get-tuple-element.31), channel_id=1, source_target_pairs={{0,1},{1,0},{2,3},{3,2},{4,5},{5,4},{6,7},{7,6},{8,9},{9,8},{10,11... | collective-permute-start | bytes 1572872 | tf_op jit(solution)/shard_map/ppermute | solution.py:75
Sparse Core Ops, SparseCore 0:
  9.4 83.0 all-gather.1

commit v7 on v6

--- a/solution.py
+++ b/solution.py
@@ -84,17 +84,18 @@
 
 
 def mix_kernel(
-    where_ref, own_ref, other_ref, residual_ref, w_own_ref, w_other_ref, out_ref, total_ref
+    where_ref, own_ref, other_ref, residual_ref, w_ref, out_ref, total_ref
 ):
     total = jnp.zeros((256, 256), jnp.float32)
-    for parts_ref, w_ref in ((own_ref, w_own_ref), (other_ref, w_other_ref)):
+    core = where_ref[0]
+    for parts_ref, owner in ((own_ref, core), (other_ref, 1 - core)):
         for i in range(0, 8, 2):
             rows = [
                 jnp.concatenate([parts_ref[i + j], parts_ref[8 + i + j]], axis=0) for j in range(2)
             ]
             total += jnp.dot(
                 jnp.concatenate(rows, axis=1),
-                w_ref[i : i + 2].reshape(256, 256),
+                w_ref[i : i + 2, owner].reshape(256, 256),
                 preferred_element_type=jnp.float32,
             )
     total_ref[...] = total
@@ -215,10 +216,6 @@
     weights = lax.all_gather(
         jnp.concatenate([w_gate, w_up, w_out], axis=1), "z", axis=0, tiled=True
     ).reshape(8, 2, 128, 1280)
-
-    def rows_of(gathered, owner, start, width):
-        part = lax.dynamic_slice(gathered, (0, owner, 0, start), (8, 1, 128, width))
-        return part.reshape(8, 128, width)
 
     product = (k_stream.astype(jnp.float32) * v_stream.astype(jnp.float32)).astype(jnp.bfloat16)
     signal = lax.all_to_all(product, ROW, split_axis=0, concat_axis=1, tiled=True)
@@ -246,8 +243,7 @@
             own,
             other,
             residual.T,
-            rows_of(weights, core, 1024, 256),
-            rows_of(weights, 1 - core, 1024, 256),
+            weights[:, :, :, 1024:],
         ),
         [((2, 256, 128), jnp.bfloat16)],
         2 * 256 * 256 * 2048,

time: 164 us -> 164 us (level)
  no operation moved by 1% of the time
where the time goes in v7:
time: 164 us; the launch traced here: 163 us
  blocking collectives  45.7 us (28%)
  starting transfers between devices  44.5 us (27%)
  waiting for transfers between devices  32.6 us (20%)
  between operations  13.8 us (8%)
  matrix products  10 us (6%)
  Pallas kernels  6.54 us (4%)
  local copies, waits for them, and re-layouts  5.27 us (3%)
  other arithmetic  4.62 us (3%)
    ppermute x4, starting transfers between devices, swap(): return lax.ppermute(array, axis, [(0, 1), (1, 0)])  21.4 us
    all_to_all x1, blocking collectives, on_device(): lax.all_to_all(spread, ('y', 'xl', 'xh'), split_axis=0, concat_axis=0, ti...  17.7 us
    all_to_all x1, starting transfers between devices, on_device(): lax.all_to_all(product, ROW, split_axis=0, concat_axis=1, tiled=True)  17 us
    all_to_all x1, blocking collectives, gather_plane(): lax.all_to_all(spread, ('xl', 'y', 'xh'), split_axis=0, concat_axis=0, ti...  15.2 us
    all_to_all x1, blocking collectives, on_device(): lax.all_to_all(down, ('xh', 'y'), split_axis=0, concat_axis=0, tiled=True)  12.8 us
    all_to_all x1, waiting for transfers between devices, on_device(): lax.all_to_all(convolved, ROW, split_axis=1, concat_axis=0, tiled=True)  12.6 us
    ppermute x4, waiting for transfers between devices, swap(): return lax.ppermute(array, axis, [(0, 1), (1, 0)])  8.51 us
    dot_general x12, matrix products, apply_last(): jnp.einsum('ckn,nm->ckm', blocks, matrix, precision=lax.Precision.HIGHEST)  7.43 us
  transfers between devices with their start and end apart: 7, of which 6 were waited for; matrix products, arithmetic and copies ran while one was open for 10% of the time, Pallas kernels for 2%

profile of v7, /device:TPU:1, one launch (start us, length us, event | category | flops | bytes accessed | tf_op | source)
XLA Modules:
  0.0 163.1 jit_solution(14556220611771125970)
XLA Ops:
  6.5 1.8 %pad_maximum_fusion = bf16[128,1280]{1,0:T(8,128)(2,1)} fusion(bf16[128,256]{1,0:T(8,128)(2,1)} %param.18, bf16[128,512]{1,0:T(8,128)(2,1)} %param.20, bf16[128,512]{1,0:T(8,128)(2,1)} %param.19), kind=kLoop, calls=%fused_computation.17 | loop fusion | flops 983040 | bytes 655360 | tf_op jit(solution)/shard_map/concatenate | solution.py:217
  8.3 0.0 all-gather.2.cloned.1.call-update
  8.3 1.5 fusion.22
  9.8 17.0 %all-to-all-start = ((bf16[32,8,128]{2,1,0:T(8,128)(2,1)}), bf16[32,8,128]{2,1,0:T(8,128)(2,1)S(1)}, u32[]{:S(2)}, u32[]{:S(2)}) async-start(bf16[32,8,128]{2,1,0:T(8,128)(2,1)} %fusion.22), calls=%async_computation | async-start | bytes 131072 | tf_op jit(solution)/shard_map/all_to_all | solution.py:221
  26.8 0.7 slice.15
  27.5 1.0 slice.16
  28.5 0.1 copy.31
  28.6 0.7 bitcast_add_fusion
  29.2 0.1 copy.26
  29.3 0.1 sine_negate_fusion.7
  29.5 0.1 maximum_bitcast_fusion
  29.6 0.5 convolution_bitcast_fusion
  30.1 0.5 convolution_bitcast_fusion.1
  30.6 0.6 fusion.26
  31.2 0.6 convolution_add_fusion.1
  31.8 0.6 fusion.38
  32.5 0.6 convolution_subtract_fusion.1
  33.1 0.0 copy-start.4
  33.1 0.0 copy-start.2
  33.1 6.3 %all-to-all-done = bf16[32,8,128]{2,1,0:T(8,128)(2,1)S(1)} async-done(((bf16[32,8,128]{2,1,0:T(8,128)(2,1)}), bf16[32,8,128]{2,1,0:T(8,128)(2,1)S(1)}, u32[]{:S(2)}, u32[]{:S(2)}) %all-to-all-start) | async-done | bytes 65568 | tf_op jit(solution)/shard_map/all_to_all | solution.py:221
  39.5 0.4 convolution_bitcast_fusion.2
  39.9 0.4 convolution_bitcast_fusion.3
  40.3 0.6 fusion.28
  40.9 0.0 copy-start.3
  40.9 0.6 fusion.40
  41.5 0.6 convolution_subtract_fusion.2
  42.1 0.7 multiply_subtract_fusion
  42.8 0.6 fusion.34
  43.4 0.6 fusion.32
  44.0 0.6 convolution_add_fusion
  44.7 0.6 convolution_subtract_fusion
  45.3 0.4 fusion.6
  45.7 0.4 fusion.2
  46.1 0.7 copy.27
  46.8 6.2 %all-to-all-start.1 = ((bf16[8,32,128]{2,0,1:T(8,128)(2,1)}), bf16[8,32,128]{2,0,1:T(8,128)(2,1)S(1)}, u32[]{:S(2)}, u32[]{:S(2)}) async-start(bf16[8,32,128]{2,0,1:T(8,128)(2,1)} %copy.27), calls=%async_computation.1 | async-start | bytes 131072 | tf_op jit(solution)/shard_map/all_to_all | solution.py:230
  53.0 12.6 %all-to-all-done.1 = bf16[8,32,128]{2,0,1:T(8,128)(2,1)S(1)} async-done(((bf16[8,32,128]{2,0,1:T(8,128)(2,1)}), bf16[8,32,128]{2,0,1:T(8,128)(2,1)S(1)}, u32[]{:S(2)}, u32[]{:S(2)}) %all-to-all-start.1) | async-done | bytes 65568 | tf_op jit(solution)/shard_map/all_to_all | solution.py:230
  65.6 0.1 copy.28
  65.8 0.1 broadcast_in_dim.7
  65.9 15.2 %all_to_all.41.own_ref = bf16[16,128,128]{2,1,0:T(8,128)(2,1)S(1)} all-to-all(bf16[16,128,128]{2,1,0:T(8,128)(2,1)S(1)} %bitcast.110), channel_id=1, replica_groups=mesh['z'=16,'xl'=2,'y'=4,'xh'=2,'core'=2] {'xl','y','xh'}, dimensions={0} | all-to-all | bytes 1048576 | tf_op jit(solution)/shard_map/all_to_all | solution.py:83
  81.1 6.0 %collective-permute-start = (bf16[16,128,128]{2,1,0:T(8,128)(2,1)S(1)}, bf16[16,128,128]{2,1,0:T(8,128)(2,1)S(1)}, u32[]{:S(2)}, u32[]{:S(2)}) collective-permute-start(bf16[16,128,128]{2,1,0:T(8,128)(2,1)S(1)} %all_to_all.41.own_ref), channel_id=1, source_target_pairs={{0,1},{1,0},{2,3},{3,2},{4,5},{5,4},{6,7},{7,6},{8,9},{9,8},{10,11... | collective-permute-start | bytes 1572872 | tf_op jit(solution)/shard_map/ppermute | solution.py:75
  87.2 0.1 copy.29
  87.3 0.1 pad_add_fusion.where_ref
  87.4 5.1 %all-gather.2.cloned.1.call-done = bf16[2048,1280]{1,0:T(8,128)(2,1)} async-done(((bf16[128,1280]{1,0:T(8,128)(2,1)}), bf16[2048,1280]{1,0:T(8,128)(2,1)}) %all-gather.2.cloned.1.call-update) | async-done | bytes 5242896 | tf_op jit(solution)/shard_map/all_gather | solution.py:216
  92.5 1.5 slice.20.w_ref
  94.0 1.0 shard_map.109
  95.0 0.2 broadcast_in_dim.8
  95.2 17.7 %all_to_all.42 = bf16[16,256,128]{2,1,0:T(8,128)(2,1)S(1)} all-to-all(bf16[16,256,128]{2,1,0:T(8,128)(2,1)S(1)} %bitcast.108), channel_id=1, replica_groups=mesh['z'=16,'xl'=2,'y'=4,'xh'=2,'core'=2] {'y','xl','xh'}, dimensions={0} | all-to-all | bytes 2097152 | tf_op jit(solution)/shard_map/all_to_all | solution.py:253
  112.9 0.1 add_convert_fusion.1
  113.1 10.0 %collective-permute-start.1 = (bf16[8,256,128]{2,1,0:T(8,128)(2,1)S(1)}, bf16[8,256,128]{2,1,0:T(8,128)(2,1)S(1)}, u32[]{:S(2)}, u32[]{:S(2)}) collective-permute-start(bf16[8,256,128]{2,1,0:T(8,128)(2,1)S(1)} %bitcast.103), channel_id=1, source_target_pairs={{0,1},{1,0},{2,3},{3,2},{4,5},{5,4},{6,7},{7,6},{8,9},{9,8},{10,11... | collective-permute-start | bytes 1572872 | tf_op jit(solution)/shard_map/ppermute | solution.py:75
  123.1 1.3 shard_map.110
  124.4 0.2 collective-permute-done.1.parts_ref
  124.6 1.0 shard_map.112
  125.6 0.0 copy-start.1
  125.6 2.2 %collective-permute-start.2 = (bf16[160,1024]{1,0:T(8,128)(2,1)S(1)}, bf16[160,1024]{1,0:T(8,128)(2,1)S(1)}, u32[]{:S(2)}, u32[]{:S(2)}) collective-permute-start(bf16[160,1024]{1,0:T(8,128)(2,1)S(1)} %shard_map.112), channel_id=1, source_target_pairs={{0,16},{16,0},{1,17},{17,1},{2,18},{18,2},{3,19},{19,3},{4,20},{20... | collective-permute-start | bytes 983048 | tf_op jit(solution)/shard_map/ppermute | solution.py:75
  127.9 1.0 shard_map.111
  128.9 7.8 %collective-permute-done.2.far_ref = bf16[160,1024]{1,0:T(8,128)(2,1)S(1)} collective-permute-done((bf16[160,1024]{1,0:T(8,128)(2,1)S(1)}, bf16[160,1024]{1,0:T(8,128)(2,1)S(1)}, u32[]{:S(2)}, u32[]{:S(2)}) %collective-permute-start.2) | collective-permute-done | bytes 327712 | tf_op jit(solution)/shard_map/ppermute | solution.py:75
  136.7 1.2 shard_map.113
  137.9 3.1 %collective-permute-start.3 = (bf16[8,128,256]{2,1,0:T(8,128)(2,1)S(1)}, bf16[8,128,256]{2,1,0:T(8,128)(2,1)S(1)}, u32[]{:S(2)}, u32[]{:S(2)}) collective-permute-start(bf16[8,128,256]{2,1,0:T(8,128)(2,1)S(1)} %get-tuple-element.31), channel_id=1, source_target_pairs={{0,1},{1,0},{2,3},{3,2},{4,5},{5,4},{6,7},{7,6},{8,9},{9,8},{10,11... | collective-permute-start | bytes 1572872 | tf_op jit(solution)/shard_map/ppermute | solution.py:75
  141.0 1.0 shard_map.114
  142.1 0.5 collective-permute-done.3
  142.5 0.1 add_convert_fusion
  142.7 12.8 %all_to_all.43 = bf16[8,128,256]{2,1,0:T(8,128)(2,1)S(1)} all-to-all(bf16[8,128,256]{2,1,0:T(8,128)(2,1)S(1)} %add_convert_fusion), channel_id=1, replica_groups=mesh['z'=16,'xl'=2,'y'=4,'xh'=2,'core'=2] {'xh','y'}, dimensions={0} | all-to-all | bytes 1048576 | tf_op jit(solution)/shard_map/all_to_all | solution.py:300
  155.5 0.1 convert_reduce_fusion
  155.6 0.7 copy.30
  (11 shorter events, 0.1 us)
Async XLA Ops:
  6.5 86.0 %all-gather.2.cloned.1.call-start = ((), (), s32[]{:S(2)}) async-start(), calls=%async_computation.5 | async-start | bytes 5570560 | tf_op jit(solution)/shard_map/all_gather | solution.py:216
  9.8 29.6 %all-to-all-start = ((bf16[32,8,128]{2,1,0:T(8,128)(2,1)}), bf16[32,8,128]{2,1,0:T(8,128)(2,1)S(1)}, u32[]{:S(2)}, u32[]{:S(2)}) async-start(bf16[32,8,128]{2,1,0:T(8,128)(2,1)} %fusion.22), calls=%async_computation | async-start | bytes 131072 | tf_op jit(solution)/shard_map/all_to_all | solution.py:221
  33.1 19.9 %copy-start.4 = (f32[4096]{0:T(1024)S(1)}, f32[4096]{0:T(1024)}, u32[]{:S(2)}) copy-start(f32[4096]{0:T(1024)} %param.17) | copy-start | bytes 49156
  33.1 32.5 %copy-start.2 = (bf16[256,128]{1,0:T(8,128)(2,1)S(1)}, bf16[256,128]{1,0:T(8,128)(2,1)}, u32[]{:S(2)}) copy-start(bf16[256,128]{1,0:T(8,128)(2,1)} %param.11) | copy-start | bytes 196612
  40.9 46.3 %copy-start.3 = (bf16[256,128]{1,0:T(8,128)(2,1)S(1)}, bf16[256,128]{1,0:T(8,128)(2,1)}, u32[]{:S(2)}) copy-start(bf16[256,128]{1,0:T(8,128)(2,1)} %param.16) | copy-start | bytes 196612
  46.8 18.8 %all-to-all-start.1 = ((bf16[8,32,128]{2,0,1:T(8,128)(2,1)}), bf16[8,32,128]{2,0,1:T(8,128)(2,1)S(1)}, u32[]{:S(2)}, u32[]{:S(2)}) async-start(bf16[8,32,128]{2,0,1:T(8,128)(2,1)} %copy.27), calls=%async_computation.1 | async-start | bytes 131072 | tf_op jit(solution)/shard_map/all_to_all | solution.py:230
  81.1 12.9 %collective-permute-start = (bf16[16,128,128]{2,1,0:T(8,128)(2,1)S(1)}, bf16[16,128,128]{2,1,0:T(8,128)(2,1)S(1)}, u32[]{:S(2)}, u32[]{:S(2)}) collective-permute-start(bf16[16,128,128]{2,1,0:T(8,128)(2,1)S(1)} %all_to_all.41.own_ref), channel_id=1, source_target_pairs={{0,1},{1,0},{2,3},{3,2},{4,5},{5,4},{6,7},{7,6},{8,9},{9,8},{10,11... | collective-permute-start | bytes 1572872 | tf_op jit(solution)/shard_map/ppermute | solution.py:75
  92.5 30.6 %copy-start = (bf16[2048,1280]{1,0:T(8,128)(2,1)S(1)}, bf16[2048,1280]{1,0:T(8,128)(2,1)}, u32[]{:S(2)}) copy-start(bf16[2048,1280]{1,0:T(8,128)(2,1)} %all-gather.2.cloned.1.call-done) | copy-start | bytes 15728644
  113.1 11.6 %collective-permute-start.1 = (bf16[8,256,128]{2,1,0:T(8,128)(2,1)S(1)}, bf16[8,256,128]{2,1,0:T(8,128)(2,1)S(1)}, u32[]{:S(2)}, u32[]{:S(2)}) collective-permute-start(bf16[8,256,128]{2,1,0:T(8,128)(2,1)S(1)} %bitcast.103), channel_id=1, source_target_pairs={{0,1},{1,0},{2,3},{3,2},{4,5},{5,4},{6,7},{7,6},{8,9},{9,8},{10,11... | collective-permute-start | bytes 1572872 | tf_op jit(solution)/shard_map/ppermute | solution.py:75
  125.6 11.1 %copy-start.1 = (bf16[512,4096]{1,0:T(8,128)(2,1)S(1)}, bf16[512,4096]{1,0:T(8,128)(2,1)}, u32[]{:S(2)}) copy-start(bf16[512,4096]{1,0:T(8,128)(2,1)} %w_ref.3) | copy-start | bytes 12582916
  125.6 11.1 %collective-permute-start.2 = (bf16[160,1024]{1,0:T(8,128)(2,1)S(1)}, bf16[160,1024]{1,0:T(8,128)(2,1)S(1)}, u32[]{:S(2)}, u32[]{:S(2)}) collective-permute-start(bf16[160,1024]{1,0:T(8,128)(2,1)S(1)} %shard_map.112), channel_id=1, source_target_pairs={{0,16},{16,0},{1,17},{17,1},{2,18},{18,2},{3,19},{19,3},{4,20},{20... | collective-permute-start | bytes 983048 | tf_op jit(solution)/shard_map/ppermute | solution.py:75
  137.9 4.6 %collective-permute-start.3 = (bf16[8,128,256]{2,1,0:T(8,128)(2,1)S(1)}, bf16[8,128,256]{2,1,0:T(8,128)(2,1)S(1)}, u32[]{:S(2)}, u32[]{:S(2)}) collective-permute-start(bf16[8,128,256]{2,1,0:T(8,128)(2,1)S(1)} %get-tuple-element.31), channel_id=1, source_target_pairs={{0,1},{1,0},{2,3},{3,2},{4,5},{5,4},{6,7},{7,6},{8,9},{9,8},{10,11... | collective-permute-start | bytes 1572872 | tf_op jit(solution)/shard_map/ppermute | solution.py:75
Sparse Core Ops, SparseCore 0:
  9.4 83.0 all-gather.1
